TPU v7x, 512 devices: a whole 4x8x8 slice. The times are simulated.
512 devices in a mesh: gx: 128 (over x, z, y_hi), gy: 4 (over y_lo, core).
Axes of the slice: x: 4, y: 8 (y_hi: 4, y_lo: 2; y = y_hi * 2 + y_lo), z: 8, core: 2. Of those that a mesh axis runs over, the one named last changes fastest.
Arguments:
- wave_sq: float32 [1024, 128, 512], P('gx', 'gy'), may hold values from 0.2 to 2
- absorb: float32 [1024, 128, 512], P('gx', 'gy'), may hold values from 0.05 to 0.5
Outputs:
- level_one: float32 [2, 3, 3, 3, 512, 64, 256], P(None, None, None, None, 'gx', 'gy')
- level_two: float32 [2, 3, 3, 3, 256, 32, 128], P(None, None, None, None, 'gx', 'gy')
- level_three: float32 [2, 3, 3, 3, 128, 16, 64], P(None, None, None, None, 'gx')
All inputs are finite; a program needn't handle non-finite values.
Results may differ from a plain program's by a relative error of at most 0.0001.
Values sent between devices are 32-bit elements; how exact they have to be, the bound alone decides.
A program may use at most 64 MiB of HBM per device.

v0:
```python
import jax
import jax.numpy as jnp
from jax import lax
from jax.sharding import PartitionSpec as P

RESTRICT = (0.25, 0.5, 0.25)


def passed_along(block, axis, distance):
    devices = range(lax.axis_size(axis))
    route = [(i - distance, i) for i in devices if i - distance in devices]
    return lax.ppermute(block, axis, route)


def spread_weight(distance):
    if distance == 0:
        return 1.0
    if abs(distance) == 1:
        return 0.5
    return 0.0


def pad_front(array, axis):
    widths = [(0, 0)] * array.ndim
    widths[axis] = (1, 0)
    return jnp.pad(array, widths)


def coarsen(stencil, offset_axis, cell_axis, anchor, extent):
    length = stencil.shape[cell_axis]
    halves = (length - 1) // 2
    pieces = [
        lax.slice_in_dim(stencil, first_cell, first_cell + 2 * halves - 1, 2, cell_axis)
        for first_cell in (0, 1, 2)
    ]
    offsets_in = stencil.shape[offset_axis]
    fine_offsets = (0,) if offsets_in == 1 else (-1, 0, 1)
    mask_shape = list(pieces[0].shape)
    mask_shape[offset_axis] = 1
    position = anchor + lax.broadcasted_iota(jnp.int32, tuple(mask_shape), cell_axis)
    blocks = []
    for coarse_off in (-1, 0, 1):
        summed = jnp.zeros(tuple(mask_shape), stencil.dtype)
        for fine_step in (-1, 0, 1):
            for fine_off in fine_offsets:
                factor = RESTRICT[fine_step + 1] * spread_weight(
                    fine_step + fine_off - 2 * coarse_off
                )
                if factor != 0.0:
                    offset_slot = 0 if offsets_in == 1 else fine_off + 1
                    summed = summed + factor * lax.slice_in_dim(
                        pieces[fine_step + 1], offset_slot, offset_slot + 1, 1, offset_axis
                    )
        inside = (position + coarse_off >= 0) & (position + coarse_off < extent)
        blocks.append(jnp.where(inside, summed, 0.0))
    return jnp.concatenate(blocks, axis=offset_axis)


def depth_table(cells, fine_off):
    half = cells // 2
    fine_place = lax.broadcasted_iota(jnp.int32, (cells, half), 0)
    coarse_place = lax.broadcasted_iota(jnp.int32, (cells, half), 1)
    columns = []
    for coarse_off in (-1, 0, 1):
        weights = jnp.zeros((cells, half), jnp.float32)
        for fine_step in (-1, 0, 1):
            factor = RESTRICT[fine_step + 1] * spread_weight(fine_step + fine_off - 2 * coarse_off)
            if factor != 0.0:
                weights = weights + jnp.where(
                    fine_place == 2 * coarse_place + fine_step, factor, 0.0
                ).astype(jnp.float32)
        inside = (coarse_place + coarse_off >= 0) & (coarse_place + coarse_off < half)
        columns.append(jnp.where(inside, weights, 0.0))
    return jnp.concatenate(columns, axis=1)


def coarsen_depth(stencil):
    cells = stencil.shape[6]
    half = cells // 2
    offsets_in = stencil.shape[3]
    fine_offsets = (0,) if offsets_in == 1 else (-1, 0, 1)
    total = None
    for fine_off in fine_offsets:
        slot = 0 if offsets_in == 1 else fine_off + 1
        slab = lax.slice_in_dim(stencil, slot, slot + 1, 1, 3)
        term = jnp.matmul(slab, depth_table(cells, fine_off), precision=lax.Precision.HIGHEST)
        total = term if total is None else total + term
    blocks = [lax.slice_in_dim(total, part * half, (part + 1) * half, 1, 6) for part in range(3)]
    return jnp.concatenate(blocks, axis=3)


def line_tables(cells):
    places = jnp.arange(cells, dtype=jnp.int32)
    lower = jnp.where(places >= 1, -1.0, 0.0).astype(jnp.float32)
    upper = jnp.where(places <= cells - 2, -1.0, 0.0).astype(jnp.float32)
    lap_line = jnp.stack([lower, jnp.full((cells,), 2.0, jnp.float32), upper])
    one_line = jnp.ones((1, cells), jnp.float32)
    tables = []
    for coarse_level in range(3):
        lap_line = coarsen(pad_front(lap_line, 1), 0, 1, 0, lap_line.shape[1] // 2)
        one_line = coarsen(pad_front(one_line, 1), 0, 1, 0, one_line.shape[1] // 2)
        tables.append((lap_line, one_line))
    return tables


def along_x(line):
    return line[:, None, None, :, None, None]


def along_y(line):
    return line[None, :, None, None, :, None]


def along_z(line):
    return line[None, None, :, None, None, :]


def assemble(stencil, lap_x, one_x, lap_y, one_y, lap_z, one_z):
    grid = along_x(lap_x) * along_y(one_y) * along_z(one_z)
    grid = grid + along_x(one_x) * along_y(lap_y) * along_z(one_z)
    grid = grid + along_x(one_x) * along_y(one_y) * along_z(lap_z)
    return jnp.stack([grid - stencil[0], -stencil[1]])


def local_slice(table, start, cells):
    return lax.dynamic_slice_in_dim(table, start, cells, 1)


def one_pass(stencil, cell_axis, whole_rows, anchor_x, extent_x, anchor_y, extent_y):
    cells = stencil.shape[cell_axis]
    if cell_axis == 4:
        last_plane = lax.slice_in_dim(stencil, cells - 1, cells, 1, 4)
        received = passed_along(last_plane, "gx", 1)
        extended = jnp.concatenate([received, stencil], axis=4)
        return coarsen(extended, 1, 4, anchor_x, extent_x)
    if cell_axis == 5 and (not whole_rows):
        last_row = lax.slice_in_dim(stencil, cells - 1, cells, 1, 5)
        received = passed_along(last_row, "gy", 1)
        extended = jnp.concatenate([received, stencil], axis=5)
        return coarsen(extended, 2, 5, anchor_y, extent_y)
    return coarsen_depth(stencil)


def local(wave_sq, absorb):
    rows_x, rows_y, depth_z = wave_sq.shape
    index_x = lax.axis_index("gx")
    index_y = lax.axis_index("gy")
    size_x = lax.axis_size("gx")
    size_y = lax.axis_size("gy")
    tables_x = line_tables(rows_x * size_x)
    tables_y = line_tables(rows_y * size_y)
    tables_z = line_tables(depth_z)
    sweep_axes = (4, 5, 6)
    stencil = jnp.stack([wave_sq + 0.5 * absorb, absorb - 0.5 * wave_sq])[:, None, None, None]
    results = []
    for coarse_level in range(3):
        whole_rows = False
        owned_x = rows_x // 2 ** (coarse_level + 1)
        owned_y = rows_y // 2 ** (coarse_level + 1)
        anchor_x = index_x * owned_x
        anchor_y = index_y * owned_y
        for cell_axis in sweep_axes:
            stencil = one_pass(
                stencil,
                cell_axis,
                whole_rows,
                anchor_x,
                owned_x * size_x,
                anchor_y,
                owned_y * size_y,
            )
        if coarse_level == 2:
            stencil = lax.all_gather(stencil, "gy", axis=5, tiled=True)
        cells_x = stencil.shape[4]
        cells_y = stencil.shape[5]
        start_y = 0 if coarse_level == 2 else index_y * cells_y
        lap_x, one_x = tables_x[coarse_level]
        lap_y, one_y = tables_y[coarse_level]
        lap_z, one_z = tables_z[coarse_level]
        lap_x = local_slice(lap_x, index_x * cells_x, cells_x)
        one_x = local_slice(one_x, index_x * cells_x, cells_x)
        lap_y = local_slice(lap_y, start_y, cells_y)
        one_y = local_slice(one_y, start_y, cells_y)
        results.append(assemble(stencil, lap_x, one_x, lap_y, one_y, lap_z, one_z))
    return (results[0], results[1], results[2])


def solution(mesh):
    return jax.shard_map(
        local,
        mesh=mesh,
        in_specs=(P("gx", "gy", None), P("gx", "gy", None)),
        out_specs=(
            P(None, None, None, None, "gx", "gy", None),
            P(None, None, None, None, "gx", "gy", None),
            P(None, None, None, None, "gx", None, None),
        ),
        check_vma=False,
    )
```

profile of v0, /device:TPU:7, one launch (start us, length us, event | category | flops | bytes accessed | tf_op | source)
XLA Modules:
  0.0 206.5 jit_solution(12861778089981783555)
XLA Ops:
  0.6 1.3 add_bitcast_fusion
  2.1 4.2 %collective-permute-start = (f32[2,1,1,1,1,32,512]{6,5,4,2,1,0,3:T(8,128)S(1)}, f32[2,1,1,1,1,32,512]{6,5,4,2,1,0,3:T(8,128)S(1)}, u32[]{:S(2)}, u32[]{:S(2)}) collective-permute-start(f32[2,1,1,1,1,32,512]{6,5,4,2,1,0,3:T(8,128)S(1)} %slice.1175), channel_id=1, source_target_pairs={{0,4},{4,8},{8,12},{12,16},{16,20},{20,24},{24,28},{28,32},{32,36}... | collective-permute-start | bytes 393224 | tf_op jit(solution)/shard_map/ppermute | solution.py:12
  19.2 0.6 compare_and_fusion.13
  20.0 0.6 compare_and_fusion.11
  21.7 0.6 compare_and_fusion.4
  22.2 0.6 add_select_fusion.13
  22.9 0.7 broadcast_multiply_fusion
  23.5 0.7 broadcast_multiply_fusion.2
  24.2 0.7 broadcast_multiply_fusion.1
  24.9 1.4 select_select_fusion.1
  26.3 1.0 fusion.54
  27.3 0.8 fusion.98
  28.6 0.6 pad_maximum_fusion.32
  30.0 4.2 %collective-permute-start.1 = (f32[2,3,1,1,4,1,512]{6,5,4,2,1,0,3:T(1,128)S(1)}, f32[2,3,1,1,4,1,512]{6,5,4,2,1,0,3:T(1,128)S(1)}, u32[]{:S(2)}, u32[]{:S(2)}) collective-permute-start(f32[2,3,1,1,4,1,512]{6,5,4,2,1,0,3:T(1,128)S(1)} %slice.1176), channel_id=1, source_target_pairs={{0,1},{1,2},{2,3},{4,5},{5,6},{6,7},{8,9},{9,10},{10,11},{12,13},{... | collective-permute-start | bytes 147464 | tf_op jit(solution)/shard_map/ppermute | solution.py:12
  34.8 2.2 %slice.941 = f32[2,3,1,1,4,16,512]{6,5,4,2,1,0,3:T(8,128)} slice(f32[2,3,1,1,4,32,512]{6,5,4,2,1,0,3:T(8,128)S(1)} %pad_maximum_fusion.3), slice={[0:2:1], [0:3:1], [0:1:1], [0:1:1], [0:4:1], [0:31:2], [0:512:1]} | slice | bytes 1572864 | tf_op jit(solution)/shard_map/slice | solution.py:33
  36.9 2.2 %slice.942 = f32[2,3,1,1,4,16,512]{6,5,4,2,1,0,3:T(8,128)} slice(f32[2,3,1,1,4,32,512]{6,5,4,2,1,0,3:T(8,128)S(1)} %pad_maximum_fusion.3), slice={[0:2:1], [0:3:1], [0:1:1], [0:1:1], [0:4:1], [1:32:2], [0:512:1]} | slice | bytes 1572864 | tf_op jit(solution)/shard_map/slice | solution.py:33
  39.1 1.6 maximum_maximum_fusion.2
  40.7 3.1 %slice.940 = f32[2,3,1,1,4,16,512]{6,5,4,2,1,0,3:T(8,128)S(1)} slice(f32[2,3,1,1,4,33,512]{6,5,4,2,1,0,3:T(8,128)} %maximum_maximum_fusion.2), slice={[0:2:1], [0:3:1], [0:1:1], [0:1:1], [0:4:1], [0:31:2], [0:512:1]} | slice | bytes 1572864 | tf_op jit(solution)/shard_map/slice | solution.py:33
  44.3 0.6 copy-done.10
  45.2 6.2 %fusion.5 = f32[2,3,3,1,4,16,768]{6,5,4,2,1,0,3:T(8,128)S(1)} fusion(f32[2,3,1,1,4,16,512]{6,5,4,2,1,0,3:T(8,128)S(1)} %get-tuple-element.32, f32[2,3,1,1,4,16,512]{6,5,4,2,1,0,3:T(8,128)S(1)} %get-tuple-element.31, f32[2,3,1,1,4,16,512]{6,5,4,2,1,0,3:T(8,128)S(1)} %get-tuple-element.30, f32[512,256]{1,0:T(8,128)S(1)} %copy-done.12, ...), kind=kOutput, calls=%fused_computation.10 | convolution fusion | flops 5437784064 | bytes 7471104 | tf_op jit(solution)/shard_map/dot_general | solution.py:86
  52.3 0.6 copy-done
  53.7 1.0 slice.1200
  54.8 4.5 %collective-permute-start.2 = (f32[2,3,3,3,1,16,256]{6,5,4,2,1,0,3:T(8,128)}, f32[2,3,3,3,1,16,256]{6,5,4,2,1,0,3:T(8,128)}, u32[]{:S(2)}, u32[]{:S(2)}) collective-permute-start(f32[2,3,3,3,1,16,256]{6,5,4,2,1,0,3:T(8,128)} %slice.1200), channel_id=1, source_target_pairs={{0,4},{4,8},{8,12},{12,16},{16,20},{20,24},{24,28},{28,32},{32,36}... | collective-permute-start | bytes 2654216 | tf_op jit(solution)/shard_map/ppermute | solution.py:12
  59.8 1.3 pad_maximum_fusion.31
  62.4 42.7 %collective-permute-done.2 = f32[2,3,3,3,1,16,256]{6,5,4,2,1,0,3:T(8,128)} collective-permute-done((f32[2,3,3,3,1,16,256]{6,5,4,2,1,0,3:T(8,128)}, f32[2,3,3,3,1,16,256]{6,5,4,2,1,0,3:T(8,128)}, u32[]{:S(2)}, u32[]{:S(2)}) %collective-permute-start.2) | collective-permute-done | bytes 884768 | tf_op jit(solution)/shard_map/ppermute | solution.py:12
  105.2 1.9 maximum_maximum_fusion
  107.7 0.7 fusion.23
  108.7 0.8 slice.1210
  109.4 2.1 %collective-permute-start.3 = (f32[2,3,3,3,2,1,256]{6,5,4,2,1,0,3:T(1,128)}, f32[2,3,3,3,2,1,256]{6,5,4,2,1,0,3:T(1,128)}, u32[]{:S(2)}, u32[]{:S(2)}) collective-permute-start(f32[2,3,3,3,2,1,256]{6,5,4,2,1,0,3:T(1,128)} %slice.1210), channel_id=1, source_target_pairs={{0,1},{1,2},{2,3},{4,5},{5,6},{6,7},{8,9},{9,10},{10,11},{12,13},{... | collective-permute-start | bytes 331784 | tf_op jit(solution)/shard_map/ppermute | solution.py:12
  112.0 2.2 %copy.14 = f32[2,3,3,3,4,16,256]{6,5,4,3,2,1,0:T(8,128)} copy(f32[2,3,3,3,4,16,256]{6,5,4,2,1,0,3:T(8,128)S(1)} %pad_maximum_fusion.1) | data formatting | bytes 7077888
  114.2 16.3 %slice.1037 = f32[2,3,3,3,2,8,256]{6,5,4,2,1,0,3:T(8,128)} slice(f32[2,3,3,3,2,16,256]{6,5,4,2,1,0,3:T(8,128)S(1)} %pad_maximum_fusion.2), slice={[0:2:1], [0:3:1], [0:3:1], [0:3:1], [0:2:1], [0:15:2], [0:256:1]} | slice | bytes 1769472 | tf_op jit(solution)/shard_map/slice | solution.py:33
  130.4 16.3 %slice.1042 = f32[2,3,3,3,2,8,256]{6,5,4,2,1,0,3:T(8,128)} slice(f32[2,3,3,3,2,16,256]{6,5,4,2,1,0,3:T(8,128)S(1)} %pad_maximum_fusion.2), slice={[0:2:1], [0:3:1], [0:3:1], [0:3:1], [0:2:1], [1:16:2], [0:256:1]} | slice | bytes 1769472 | tf_op jit(solution)/shard_map/slice | solution.py:33
  146.7 2.8 %maximum_maximum_fusion.1 = f32[2,3,3,3,2,17,256]{6,5,4,2,1,0,3:T(8,128)} fusion(f32[2,1,3,3,2,16,256]{6,5,4,2,1,0,3:T(8,128)S(1)} %get-tuple-element.14, f32[2,1,3,3,2,16,256]{6,5,4,2,1,0,3:T(8,128)S(1)} %get-tuple-element.13, f32[2,1,3,3,2,16,256]{6,5,4,2,1,0,3:T(8,128)S(1)} %get-tuple-element.12, f32[2,3,3,3,2,1,256]{6,5,4,2,1,0,3:T(1,128)} %collective-permute-done.3), kind=kLoop, calls=%fused_computation.3 | loop fusion | flops 1410048 | bytes 3760128 | tf_op jit(solution)/shard_map/concatenate | solution.py:139
  149.5 20.9 %slice.1034 = f32[2,3,3,3,2,8,256]{6,5,4,2,1,0,3:T(8,128)S(1)} slice(f32[2,3,3,3,2,17,256]{6,5,4,2,1,0,3:T(8,128)} %maximum_maximum_fusion.1), slice={[0:2:1], [0:3:1], [0:3:1], [0:3:1], [0:2:1], [0:15:2], [0:256:1]} | slice | bytes 1769472 | tf_op jit(solution)/shard_map/slice | solution.py:33
  171.1 0.7 copy-done.18
  171.9 0.6 fusion.27
  172.6 0.6 convolution_add_fusion.1
  173.3 0.6 fusion.10
  174.0 1.9 collective-permute-start.4
  176.1 11.2 %collective-permute-done.4 = f32[2,3,3,3,1,8,128]{6,5,4,2,1,0,3:T(8,128)S(1)} collective-permute-done((f32[2,3,3,3,1,8,128]{6,5,4,2,1,0,3:T(8,128)S(1)}, f32[2,3,3,3,1,8,128]{6,5,4,2,1,0,3:T(8,128)S(1)}, u32[]{:S(2)}, u32[]{:S(2)}) %collective-permute-start.4) | collective-permute-done | bytes 221216 | tf_op jit(solution)/shard_map/ppermute | solution.py:12
  187.4 1.9 collective-permute-start.5
  189.5 0.8 copy.15
  190.2 1.3 slice.1140
  191.6 1.6 slice.1145
  193.2 1.4 slice.1137
  196.1 8.5 %all_gather.3 = f32[2,3,3,3,1,16,64]{6,0,4,3,2,1,5:T(2,128)S(1)} all-gather(f32[2,3,3,3,1,4,64]{6,0,4,3,2,1,5:T(2,128)S(1)} %copy.13), channel_id=1, replica_groups=mesh['gx'=128,'gy'=4] {'gy'}, dimensions={5}, use_global_device_ids=true | all-gather | bytes 276480 | tf_op jit(solution)/shard_map/all_gather | solution.py:173
  204.6 0.6 slice_subtract_fusion.1
  205.7 0.8 copy.16
  (286 shorter events, 24.0 us)
Async XLA Ops:
  2.1 27.1 %collective-permute-start = (f32[2,1,1,1,1,32,512]{6,5,4,2,1,0,3:T(8,128)S(1)}, f32[2,1,1,1,1,32,512]{6,5,4,2,1,0,3:T(8,128)S(1)}, u32[]{:S(2)}, u32[]{:S(2)}) collective-permute-start(f32[2,1,1,1,1,32,512]{6,5,4,2,1,0,3:T(8,128)S(1)} %slice.1175), channel_id=1, source_target_pairs={{0,4},{4,8},{8,12},{12,16},{16,20},{20,24},{24,28},{28,32},{32,36}... | collective-permute-start | bytes 393224 | tf_op jit(solution)/shard_map/ppermute | solution.py:12
  17.9 11.5 %copy-start.32 = (f32[3,256]{1,0:T(4,128)}, f32[3,256]{1,0:T(4,128)S(1)}, u32[]{:S(2)}) copy-start(f32[3,256]{1,0:T(4,128)S(1)} %pad_maximum_fusion.16) | copy-start | bytes 9220
  18.7 2.8 %copy-start.36 = (f32[3,128]{1,0:T(4,128)}, f32[3,128]{1,0:T(4,128)S(1)}, u32[]{:S(2)}) copy-start(f32[3,128]{1,0:T(4,128)S(1)} %pad_maximum_fusion.25) | copy-start | bytes 4612
  30.0 9.1 %collective-permute-start.1 = (f32[2,3,1,1,4,1,512]{6,5,4,2,1,0,3:T(1,128)S(1)}, f32[2,3,1,1,4,1,512]{6,5,4,2,1,0,3:T(1,128)S(1)}, u32[]{:S(2)}, u32[]{:S(2)}) collective-permute-start(f32[2,3,1,1,4,1,512]{6,5,4,2,1,0,3:T(1,128)S(1)} %slice.1176), channel_id=1, source_target_pairs={{0,1},{1,2},{2,3},{4,5},{5,6},{6,7},{8,9},{9,10},{10,11},{12,13},{... | collective-permute-start | bytes 147464 | tf_op jit(solution)/shard_map/ppermute | solution.py:12
  39.1 4.7 %copy-start.8 = (f32[2,3,1,1,4,16,512]{6,5,4,2,1,0,3:T(8,128)S(1)}, f32[2,3,1,1,4,16,512]{6,5,4,2,1,0,3:T(8,128)}, u32[]{:S(2)}) copy-start(f32[2,3,1,1,4,16,512]{6,5,4,2,1,0,3:T(8,128)} %slice.941) | copy-start | bytes 2359300
  39.1 4.7 %copy-start.9 = (f32[2,3,1,1,4,16,512]{6,5,4,2,1,0,3:T(8,128)S(1)}, f32[2,3,1,1,4,16,512]{6,5,4,2,1,0,3:T(8,128)}, u32[]{:S(2)}) copy-start(f32[2,3,1,1,4,16,512]{6,5,4,2,1,0,3:T(8,128)} %slice.942) | copy-start | bytes 2359300
  43.8 1.0 copy-start.10
  43.8 1.2 copy-start.11
  43.9 1.3 copy-start.12
  51.9 1.0 copy-start
  51.9 1.4 copy-start.2
  51.9 1.8 copy-start.4
  54.8 50.4 %collective-permute-start.2 = (f32[2,3,3,3,1,16,256]{6,5,4,2,1,0,3:T(8,128)}, f32[2,3,3,3,1,16,256]{6,5,4,2,1,0,3:T(8,128)}, u32[]{:S(2)}, u32[]{:S(2)}) collective-permute-start(f32[2,3,3,3,1,16,256]{6,5,4,2,1,0,3:T(8,128)} %slice.1200), channel_id=1, source_target_pairs={{0,4},{4,8},{8,12},{12,16},{16,20},{20,24},{24,28},{28,32},{32,36}... | collective-permute-start | bytes 2654216 | tf_op jit(solution)/shard_map/ppermute | solution.py:12
  61.8 43.3 %copy-start.1 = (f32[2,3,3,1,4,16,256]{6,5,4,2,1,0,3:T(8,128)S(1)}, f32[2,3,3,1,4,16,256]{6,5,4,2,1,0,3:T(8,128)}, u32[]{:S(2)}) copy-start(f32[2,3,3,1,4,16,256]{6,5,4,2,1,0,3:T(8,128)} %copy-done) | copy-start | bytes 3538948
  61.8 43.3 %copy-start.3 = (f32[2,3,3,1,4,16,256]{6,5,4,2,1,0,3:T(8,128)S(1)}, f32[2,3,3,1,4,16,256]{6,5,4,2,1,0,3:T(8,128)}, u32[]{:S(2)}) copy-start(f32[2,3,3,1,4,16,256]{6,5,4,2,1,0,3:T(8,128)} %copy-done.2) | copy-start | bytes 3538948
  61.8 43.3 %copy-start.5 = (f32[2,3,3,1,4,16,256]{6,5,4,2,1,0,3:T(8,128)S(1)}, f32[2,3,3,1,4,16,256]{6,5,4,2,1,0,3:T(8,128)}, u32[]{:S(2)}) copy-start(f32[2,3,3,1,4,16,256]{6,5,4,2,1,0,3:T(8,128)} %copy-done.4) | copy-start | bytes 3538948
  109.4 37.3 %collective-permute-start.3 = (f32[2,3,3,3,2,1,256]{6,5,4,2,1,0,3:T(1,128)}, f32[2,3,3,3,2,1,256]{6,5,4,2,1,0,3:T(1,128)}, u32[]{:S(2)}, u32[]{:S(2)}) collective-permute-start(f32[2,3,3,3,2,1,256]{6,5,4,2,1,0,3:T(1,128)} %slice.1210), channel_id=1, source_target_pairs={{0,1},{1,2},{2,3},{4,5},{5,6},{6,7},{8,9},{9,10},{10,11},{12,13},{... | collective-permute-start | bytes 331784 | tf_op jit(solution)/shard_map/ppermute | solution.py:12
  149.5 21.0 %copy-start.6 = (f32[2,3,3,3,2,8,256]{6,5,4,2,1,0,3:T(8,128)S(1)}, f32[2,3,3,3,2,8,256]{6,5,4,2,1,0,3:T(8,128)}, u32[]{:S(2)}) copy-start(f32[2,3,3,3,2,8,256]{6,5,4,2,1,0,3:T(8,128)} %slice.1037) | copy-start | bytes 2654212
  149.5 21.0 %copy-start.7 = (f32[2,3,3,3,2,8,256]{6,5,4,2,1,0,3:T(8,128)S(1)}, f32[2,3,3,3,2,8,256]{6,5,4,2,1,0,3:T(8,128)}, u32[]{:S(2)}) copy-start(f32[2,3,3,3,2,8,256]{6,5,4,2,1,0,3:T(8,128)} %slice.1042) | copy-start | bytes 2654212
  149.5 21.0 %copy-start.40 = (pred[8]{0:T(512)(128)(4,1)S(1)}, pred[8]{0:T(512)(128)(4,1)}, u32[]{:S(2)}) copy-start(pred[8]{0:T(512)(128)(4,1)} %get-tuple-element.135) | copy-start | bytes 28
  149.5 21.0 %copy-start.41 = (pred[8]{0:T(512)(128)(4,1)S(1)}, pred[8]{0:T(512)(128)(4,1)}, u32[]{:S(2)}) copy-start(pred[8]{0:T(512)(128)(4,1)} %get-tuple-element.136) | copy-start | bytes 28
  149.5 21.0 %copy-start.44 = (pred[8]{0:T(512)(128)(4,1)S(1)}, pred[8]{0:T(512)(128)(4,1)}, u32[]{:S(2)}) copy-start(pred[8]{0:T(512)(128)(4,1)} %compare_and_fusion.16) | copy-start | bytes 28
  170.9 0.9 copy-start.18
  170.9 1.0 copy-start.19
  170.9 1.6 copy-start.15
  170.9 1.6 copy-start.16
  171.0 1.6 copy-start.17
  171.0 2.2 %copy-start.13 = (f32[256,128]{1,0:T(8,128)S(1)}, f32[256,128]{1,0:T(8,128)}, u32[]{:S(2)}) copy-start(f32[256,128]{1,0:T(8,128)} %get-tuple-element.107) | copy-start | bytes 393220
  171.0 2.2 %copy-start.14 = (f32[256,128]{1,0:T(8,128)S(1)}, f32[256,128]{1,0:T(8,128)}, u32[]{:S(2)}) copy-start(f32[256,128]{1,0:T(8,128)} %get-tuple-element.110) | copy-start | bytes 393220
  173.2 2.7 %copy-start.31 = (f32[3,3,2,8]{3,2,1,0:T(2,128)S(1)}, f32[3,3,2,8]{3,2,1,0:T(2,128)}, u32[]{:S(2)}) copy-start(f32[3,3,2,8]{3,2,1,0:T(2,128)} %get-tuple-element.85) | copy-start | bytes 1732
  173.2 2.7 %copy-start.35 = (f32[3,128]{1,0:T(4,128)S(1)}, f32[3,128]{1,0:T(4,128)}, u32[]{:S(2)}) copy-start(f32[3,128]{1,0:T(4,128)} %copy-done.34) | copy-start | bytes 4612
  173.3 2.7 %copy-start.37 = (f32[3,128]{1,0:T(4,128)S(1)}, f32[3,128]{1,0:T(4,128)}, u32[]{:S(2)}) copy-start(f32[3,128]{1,0:T(4,128)} %copy-done.36) | copy-start | bytes 4612
  174.0 13.2 %collective-permute-start.4 = (f32[2,3,3,3,1,8,128]{6,5,4,2,1,0,3:T(8,128)S(1)}, f32[2,3,3,3,1,8,128]{6,5,4,2,1,0,3:T(8,128)S(1)}, u32[]{:S(2)}, u32[]{:S(2)}) collective-permute-start(f32[2,3,3,3,1,8,128]{6,5,4,2,1,0,3:T(8,128)S(1)} %slice.1228), channel_id=1, source_target_pairs={{0,4},{4,8},{8,12},{12,16},{16,20},{20,24},{24,28},{28,32},{32,36}... | collective-permute-start | bytes 663560 | tf_op jit(solution)/shard_map/ppermute | solution.py:12
  187.3 7.3 %copy-start.46 = (pred[4]{0:T(512)(128)(4,1)S(1)}, pred[4]{0:T(512)(128)(4,1)}, u32[]{:S(2)}) copy-start(pred[4]{0:T(512)(128)(4,1)} %get-tuple-element.131) | copy-start | bytes 16
  187.3 7.3 %copy-start.47 = (pred[4]{0:T(512)(128)(4,1)S(1)}, pred[4]{0:T(512)(128)(4,1)}, u32[]{:S(2)}) copy-start(pred[4]{0:T(512)(128)(4,1)} %get-tuple-element.132) | copy-start | bytes 16
  187.3 7.3 %copy-start.48 = (pred[4]{0:T(512)(128)(4,1)S(1)}, pred[4]{0:T(512)(128)(4,1)}, u32[]{:S(2)}) copy-start(pred[4]{0:T(512)(128)(4,1)} %compare_and_fusion.6) | copy-start | bytes 16
  187.4 5.8 %collective-permute-start.5 = (f32[2,3,3,3,1,1,128]{6,5,4,2,1,0,3:T(1,128)S(1)}, f32[2,3,3,3,1,1,128]{6,5,4,2,1,0,3:T(1,128)S(1)}, u32[]{:S(2)}, u32[]{:S(2)}) collective-permute-start(f32[2,3,3,3,1,1,128]{6,5,4,2,1,0,3:T(1,128)S(1)} %slice.1238), channel_id=1, source_target_pairs={{0,1},{1,2},{2,3},{4,5},{5,6},{6,7},{8,9},{9,10},{10,11},{12,13},{... | collective-permute-start | bytes 82952 | tf_op jit(solution)/shard_map/ppermute | solution.py:12
  189.3 5.5 %copy-start.25 = (f32[128,64]{0,1:T(8,128)S(1)}, f32[128,64]{0,1:T(8,128)}, u32[]{:S(2)}) copy-start(f32[128,64]{0,1:T(8,128)} %get-tuple-element.106) | copy-start | bytes 98308
  189.4 5.5 %copy-start.26 = (f32[128,64]{0,1:T(8,128)S(1)}, f32[128,64]{0,1:T(8,128)}, u32[]{:S(2)}) copy-start(f32[128,64]{0,1:T(8,128)} %get-tuple-element.114) | copy-start | bytes 98308
  189.4 5.7 %copy-start.22 = (f32[128,64]{0,1:T(8,128)S(1)}, f32[128,64]{0,1:T(8,128)}, u32[]{:S(2)}) copy-start(f32[128,64]{0,1:T(8,128)} %get-tuple-element.105) | copy-start | bytes 98308
  189.4 5.7 %copy-start.23 = (f32[128,64]{0,1:T(8,128)S(1)}, f32[128,64]{0,1:T(8,128)}, u32[]{:S(2)}) copy-start(f32[128,64]{0,1:T(8,128)} %get-tuple-element.113) | copy-start | bytes 98308
  189.4 5.7 %copy-start.24 = (f32[128,64]{0,1:T(8,128)S(1)}, f32[128,64]{0,1:T(8,128)}, u32[]{:S(2)}) copy-start(f32[128,64]{0,1:T(8,128)} %get-tuple-element.115) | copy-start | bytes 98308
  189.4 6.1 %copy-start.20 = (f32[128,64]{0,1:T(8,128)S(1)}, f32[128,64]{0,1:T(8,128)}, u32[]{:S(2)}) copy-start(f32[128,64]{0,1:T(8,128)} %get-tuple-element.104) | copy-start | bytes 98308
  189.4 6.1 %copy-start.21 = (f32[128,64]{0,1:T(8,128)S(1)}, f32[128,64]{0,1:T(8,128)}, u32[]{:S(2)}) copy-start(f32[128,64]{0,1:T(8,128)} %get-tuple-element.112) | copy-start | bytes 98308
  193.1 11.5 %copy-start.27 = (f32[3,3,16]{1,0,2:T(4,128)S(1)}, f32[3,3,16]{1,0,2:T(4,128)}, u32[]{:S(2)}) copy-start(f32[3,3,16]{1,0,2:T(4,128)} %get-tuple-element.52) | copy-start | bytes 1732
  193.1 11.4 %copy-start.28 = (f32[3,3,16]{1,0,2:T(4,128)S(1)}, f32[3,3,16]{1,0,2:T(4,128)}, u32[]{:S(2)}) copy-start(f32[3,3,16]{1,0,2:T(4,128)} %get-tuple-element.53) | copy-start | bytes 1732
  193.1 11.4 %copy-start.38 = (f32[3,64]{1,0:T(4,128)S(1)}, f32[3,64]{1,0:T(4,128)}, u32[]{:S(2)}) copy-start(f32[3,64]{1,0:T(4,128)} %pad_maximum_fusion.32) | copy-start | bytes 2308
  193.2 11.4 %copy-start.39 = (f32[3,64]{1,0:T(4,128)S(1)}, f32[3,64]{1,0:T(4,128)}, u32[]{:S(2)}) copy-start(f32[3,64]{1,0:T(4,128)} %pad_maximum_fusion.31) | copy-start | bytes 2308
  (7 other events, 4.8 us)
where the time goes:
time: 209 us; the launch traced here: 207 us
  local copies, waits for them, and re-layouts  89.1 us (43%)
  waiting for transfers between devices  53.9 us (26%)
  other arithmetic  24.9 us (12%)
  starting transfers between devices  18.9 us (9%)
  matrix products  9.16 us (4%)
  blocking collectives  8.5 us (4%)
    slice x65, local copies, waits for them, and re-layouts, coarsen(): lax.slice_in_dim(stencil, first_cell, first_cell + 2 * halves - 1, 2, cel...  76.1 us
    ppermute x6, waiting for transfers between devices, passed_along(): return lax.ppermute(block, axis, route)  53.9 us
    ppermute x6, starting transfers between devices, passed_along(): return lax.ppermute(block, axis, route)  18.9 us
    dot_general x7, matrix products, coarsen_depth(): jnp.matmul(slab, depth_table(cells, fine_off), precision=lax.Precision.HI...  9.16 us
    all_gather x1, blocking collectives, local(): stencil = lax.all_gather(stencil, 'gy', axis=5, tiled=True)  8.5 us
    unnamed x101, local copies, waits for them, and re-layouts  7.86 us
    concatenate x3, other arithmetic, one_pass(): extended = jnp.concatenate([received, stencil], axis=5)  4.44 us
  transfers between devices with their start and end apart: 6, of which 2 were waited for; matrix products, arithmetic and copies ran while one was open for 33% of the time, Pallas kernels for 0%

commit v1 on v0

v1 whole, which is shorter than its diff:
```python
import functools

import jax
import jax.numpy as jnp
import ml_dtypes
import numpy as np
from jax import lax
from jax.experimental import pallas as pl
from jax.experimental.pallas import tpu as pltpu
from jax.sharding import PartitionSpec as P

MESH = pl.DeviceIdType.MESH
BF16 = jnp.bfloat16
F32 = jnp.float32
FIRST, MIDDLE, LAST = 0, 1, 2


def hat(distance, width):
    return np.maximum(0.0, 1.0 - np.abs(distance) / width)


def line_weights(cells, level, place):
    width = 2**level
    coarse = cells // width
    fine = np.arange(cells)[None, :]
    node = width * np.arange(coarse)[:, None]
    table = np.stack([hat(fine - node, width) * hat(fine - node - a * width, width) for a in (-1, 0, 1)])
    table /= width
    if place == LAST:
        table[2, -1] = 0.0
    return table


def tail_weights(cells, level, place):
    width = 2**level
    distance = np.arange(cells) - cells
    table = np.stack([hat(distance, width) * hat(distance + width, width), hat(distance, width) ** 2]) / width
    return table * (place != LAST)


def grid_tables(cells):
    lap = np.zeros((cells, 3))
    lap[:] = (-1.0, 2.0, -1.0)
    lap[0, 0] = lap[-1, 2] = 0.0
    one = np.zeros((cells, 3))
    one[:, 1] = 1.0

    def coarsen(band):
        coarse = band.shape[0] // 2
        out = np.zeros((coarse, 3))
        for row in range(coarse):
            for a in (-1, 0, 1):
                if not 0 <= row + a < coarse:
                    continue
                for step, weight in ((-1, 0.25), (0, 0.5), (1, 0.25)):
                    fine = 2 * row + step
                    if fine < 0:
                        continue
                    for b in (-1, 0, 1):
                        distance = abs(fine + b - 2 * (row + a))
                        spread = 1.0 if distance == 0 else 0.5 if distance == 1 else 0.0
                        out[row, a + 1] += weight * spread * band[fine, b + 1]
        return out

    tables = []
    for _ in range(3):
        lap, one = coarsen(lap), coarsen(one)
        tables.append((lap.T, one.T))
    return tables


def two_terms(table):
    high = table.astype(ml_dtypes.bfloat16).astype(np.float64)
    return high, table - high


def row_features(lap, one):
    (lh, ll), (oh, ol) = two_terms(lap), two_terms(one)
    columns = [lh, lh, ll, ll, oh, oh, ol, ol]
    return np.stack(columns + [np.zeros_like(lh)] * 8, axis=1)


def column_features(lap, one):
    (lh, ll), (oh, ol) = two_terms(lap), two_terms(one)
    rows = [oh, ol, oh, ol, lh, ll, lh, ll]
    return np.stack(rows + [np.zeros_like(lh)] * 8, axis=0)


def place_slice(table, place, cells):
    whole = table.shape[1]
    start = {FIRST: 0, MIDDLE: cells, LAST: whole - cells}[place]
    return table[:, start : start + cells]


def grid_rows(grid_x, grid_y, place_x, place_y, cells_x, cells_y):
    lap_x, one_x = (place_slice(t, place_x, cells_x)[:, None, :, None] for t in grid_x)
    lap_y, one_y = (place_slice(t, place_y, cells_y)[None, :, None, :] for t in grid_y)
    lap = (lap_x * one_y + one_x * lap_y).reshape(-1)
    one = (one_x * one_y).reshape(-1)
    return row_features(lap, one)


def padded(rows, count, width=None):
    out = np.zeros((count, rows.shape[1] if width is None else width))
    out[: rows.shape[0], : rows.shape[1]] = rows
    return out


def pair(left, right):
    both = np.einsum("aJi,bKj->abJKij", left, right)
    return both.reshape(-1, left.shape[2] * right.shape[2])


def xy_tables(nx, ny, sx, sy):
    grid_x, grid_y = grid_tables(nx * sx), grid_tables(ny * sy)
    first, later = [], []
    for px in (FIRST, MIDDLE, LAST):
        for py in (FIRST, MIDDLE, LAST):
            wx = [line_weights(nx, k, px) for k in (1, 2, 3)]
            wy = [line_weights(ny, k, py) for k in (1, 2, 3)]
            tx = [tail_weights(nx, k, px)[:, None, :] for k in (1, 2, 3)]
            ty = [tail_weights(ny, k, py)[:, None, :] for k in (1, 2, 3)]

            own = pair(wx[0], wy[0])
            head_x = np.zeros((3, nx // 2, 1))
            head_x[0:2, 0, 0] = 0.125 * (px != FIRST)
            head_y = np.zeros((3, ny // 2, 1))
            head_y[0:2, 0, 0] = 0.125 * (py != FIRST)
            halo = np.concatenate([pair(head_x, wy[0]), pair(wx[0], head_y), pair(head_x, head_y)], axis=1)
            halo = padded(halo, halo.shape[0], HALO)
            grid = grid_rows(grid_x[0], grid_y[0], px, py, nx // 2, ny // 2)
            first.append(padded(np.concatenate([own, halo, halo, grid], axis=1), own.shape[0], nx * ny + 128))

            m, n = nx // 4, ny // 4
            own = pair(wx[1], wy[1])
            send = [pair(tx[1], wy[1][1:]), pair(wx[1][1:], ty[1]), pair(tx[1], ty[1])]
            rows2 = padded(np.concatenate([own, *send]), 192)
            take = np.zeros((3, 3, m, n, HALO))
            for a in range(2):
                for j in range(n):
                    take[a, 1, 0, j, a * 2 * n + j] = 1.0
                    take[a, 2, 0, j, a * 2 * n + n + j] = 1.0
                    if j + 1 < n:
                        take[a, 0, 0, j + 1, a * 2 * n + n + j] = 1.0
                for i in range(m):
                    own_e, own_f = 4 * n + a * m + i, 4 * n + (2 + a) * m + i
                    take[1, a, i, 0, own_e] = 1.0
                    take[2, a, i, 0, own_f] = 1.0
                    if i + 1 < m:
                        take[0, a, i + 1, 0, own_f] = 1.0
                for b in range(2):
                    take[a, b, 0, 0, 4 * n + 4 * m + 2 * a + b] = 1.0
            take = take.reshape(-1, HALO)
            grid = grid_rows(grid_x[1], grid_y[1], px, py, m, n)
            take2 = np.concatenate([take, take, grid], axis=1)

            n = ny // 8
            own = padded(pair(wx[2], wy[2][1:]), 32)
            send = [pair(tx[2], wy[2][1:]), pair(wx[2][1:], ty[2]), pair(tx[2], ty[2])]
            rows3 = padded(np.concatenate([own, *send]), 64)
            take = np.zeros((3, 2, n, 32))
            for a in range(2):
                for e in range(2):
                    for j in range(n):
                        take[a, e, j, (a * 2 + e) * n + j] = 1.0
                take[1 + a, 0, 0, 4 * n + 2 * a + 1] = 1.0
                take[a, 0, 0, 4 * n + 4 + 2 * a + 1] = 1.0
            take = take.reshape(-1, 32)
            grid = grid_rows(grid_x[2], grid_y[2], px, py, 1, n).reshape(3, 3, n, 16)[:, 1:].reshape(-1, 16)
            take3 = np.concatenate([take, take, grid], axis=1)

            table = np.zeros((320, nx * ny + 128))
            high, low = two_terms(rows3)
            table[:, : nx * ny] = np.concatenate([rows2, high, low])
            table[: take2.shape[0], nx * ny : nx * ny + take2.shape[1]] = take2
            table[192 : 192 + take3.shape[0], nx * ny : nx * ny + take3.shape[1]] = take3
            later.append(table)
    return np.stack(first), np.stack(later)


def z_tables(nz):
    grid = grid_tables(nz)
    half = nz // 2
    blocks = []
    one = line_weights(nz, 1, LAST)
    one[0, 0] = 0.0
    for a in range(3):
        blocks.append(np.concatenate([one[a].T, column_features(grid[0][0][a], grid[0][1][a])]))
    for k in (2, 3):
        table = line_weights(nz, k, LAST)
        columns = [
            np.concatenate([table[a].T, column_features(grid[k - 1][0][a], grid[k - 1][1][a])]) for a in (1, 2)
        ]
        block = np.concatenate(columns, axis=1)
        blocks.append(padded(block, nz + 16, half))
    return np.stack(blocks)


def gather_table(parts, n):
    table = np.zeros((3, 3, parts * n, parts, 3, 2, n))
    for a in range(3):
        for g in range(parts):
            for j in range(n):
                row = g * n + j
                table[a, 1, row, g, a, 0, j] = 1.0
                table[a, 2, row, g, a, 1, j] = 1.0
                if row + 1 < parts * n:
                    table[a, 0, row + 1, g, a, 1, j] = 1.0
    table = table.reshape(9 * parts * n, -1)
    return np.concatenate([table, table], axis=1)


HALO = 48


def split(value):
    high = value.astype(BF16)
    return high, (value - high.astype(F32)).astype(BF16)


def dot(left, right):
    return jnp.dot(left, right, preferred_element_type=F32)


def exact_dot(left, value):
    high, low = split(value)
    return dot(left, high) + dot(left, low)


def halo_kernel(
    sx, sy,
    w_hbm, a_hbm, first_hbm, later_hbm, z_hbm, gather_hbm,
    one_ref, two_ref, three_ref,
    w_ref, a_ref, first_ref, later_ref, z_ref, gather_ref,
    mass, plane, row_send, row_got, corner_send, corner_got,
    x2_send, x2_got, x3_send, x3_got, blocks, t2, t3, k2, k3, raw,
    load_sem, send_sem, got_sem,
):
    ix, iy = lax.axis_index("gx"), lax.axis_index("gy")
    nx, ny, nz = w_hbm.shape
    cells = nx * ny
    next_x, last_x = lax.rem(ix + 1, sx), lax.rem(ix + sx - 1, sx)
    next_y, last_y = lax.rem(iy + 1, sy), lax.rem(iy + sy - 1, sy)
    peers = [lax.rem(iy + step, sy) for step in range(1, sy)]

    place_x = jnp.where(ix == 0, FIRST, jnp.where(ix == sx - 1, LAST, MIDDLE))
    place_y = jnp.where(iy == 0, FIRST, jnp.where(iy == sy - 1, LAST, MIDDLE))
    place = place_x * 3 + place_y
    loads = [
        pltpu.make_async_copy(src, dst, load_sem.at[i])
        for i, (src, dst) in enumerate(
            (
                (w_hbm, w_ref),
                (a_hbm, a_ref),
                (later_hbm.at[place], later_ref),
                (z_hbm.at[pl.ds(3, 2)], z_ref.at[pl.ds(3, 2)]),
                (z_hbm.at[pl.ds(0, 3)], z_ref.at[pl.ds(0, 3)]),
                (first_hbm.at[place], first_ref),
                (gather_hbm, gather_ref),
            )
        )
    ]
    for load in loads:
        load.start()

    barrier = pltpu.get_barrier_semaphore()
    sources = [(last_x, iy), (last_x, last_y)] + [(ix, p) for p in peers]
    for device in sources:
        pl.semaphore_signal(barrier, inc=1, device_id=device, device_id_type=MESH)
    pl.semaphore_wait(barrier, len(sources))

    def send(slot, src, dst, device):
        copy = pltpu.make_async_remote_copy(
            src_ref=src, dst_ref=dst, send_sem=send_sem.at[slot], recv_sem=got_sem.at[slot],
            device_id=device, device_id_type=MESH,
        )
        copy.start()
        return copy

    plane_w = send(0, w_hbm.at[nx - 1], plane.at[0], (next_x, iy))
    plane_a = send(1, a_hbm.at[nx - 1], plane.at[1], (next_x, iy))

    loads[0].wait()
    loads[1].wait()
    for x in range(nx):
        w, a = w_ref[x], a_ref[x]
        for part, value in enumerate((-(w + 0.5 * a), 0.5 * w - a)):
            high, low = split(value)
            mass[part, 0, x * ny : (x + 1) * ny] = high
            mass[part, 1, x * ny : (x + 1) * ny] = low
            for c in range(nz // 128):
                raw[part, c, x : x + 1] = value[ny - 1 : ny, c * 128 : (c + 1) * 128]
    loads[2].wait()
    loads[3].wait()

    for part in range(2):
        table = later_ref[:, 0:cells]
        rows = dot(table, mass[part, 0]) + dot(table, mass[part, 1])
        high, low = split(rows[0:192])
        two = dot(high, z_ref[3, 0:nz]) + dot(low, z_ref[3, 0:nz])
        high, low = split(rows[192:256] + rows[256:320])
        three = dot(high, z_ref[4, 0:nz, 0:128]) + dot(low, z_ref[4, 0:nz, 0:128])
        t2[part] = two[0:144]
        t3[part] = three[0:32]
        x3_send[part * 16 : part * 16 + 16] = three[32:48]
        x2_send[part * 32 : part * 32 + 32] = two[144:176]
        for e in range(2):
            row_send[64 + e * 16 + part * 8 : 64 + e * 16 + part * 8 + 8] = two[176:184, e * 128 : e * 128 + 128]
            corner_send[8 + e * 8 + part * 4 : 8 + e * 8 + part * 4 + 4] = two[184:188, e * 128 : e * 128 + 128]
        row_send[96 + part * 4 : 96 + part * 4 + 4] = three[48:52]
        corner_send[24 + part * 4 : 24 + part * 4 + 4] = three[52:56]
        for c in range(nz // 128):
            row_send[part * 32 + c * 8 : part * 32 + c * 8 + 8] = raw[part, c]
            corner_send[part * 4 + c : part * 4 + c + 1] = raw[part, c, nx - 1 : nx]

    x3 = send(2, x3_send, x3_got, (next_x, iy))
    x2 = send(3, x2_send, x2_got, (next_x, iy))
    row = send(4, row_send, row_got, (ix, next_y))
    corner = send(5, corner_send, corner_got, (next_x, next_y))

    loads[4].wait()
    loads[5].wait()

    def own_level_one(i, carry):
        part, a = i // 3, lax.rem(i, 3)
        table = z_ref[a]
        z = dot(mass[part, 0], table[0:nz]) + dot(mass[part, 1], table[0:nz])
        high, low = split(z)
        grid = jnp.where(part == 0, table[nz : nz + 16], jnp.zeros((16, nz // 2), BF16))
        rest = jnp.concatenate([jnp.zeros((2 * HALO, nz // 2), BF16), grid, jnp.zeros((16, nz // 2), BF16)], axis=0)
        for ax in range(3):
            rows = first_ref[ax * 192 : ax * 192 + 192]
            out = dot(rows[:, 0:cells], high) + dot(rows[:, 0:cells], low) + dot(rows[:, cells:], rest)
            one_ref[part, ax, :, a] = out.reshape(3, nx // 2, ny // 2, nz // 2)
        return carry

    lax.fori_loop(0, 6, own_level_one, 0)

    row.wait_recv()
    corner.wait_recv()
    x3.wait_recv()
    for part in range(2):
        k3[part, 0:16] = x3_got[part * 16 : part * 16 + 16]
        k3[part, 16:20] = row_got[96 + part * 4 : 96 + part * 4 + 4]
        k3[part, 20:24] = corner_got[24 + part * 4 : 24 + part * 4 + 4]
        k3[part, 24:32] = jnp.zeros((8, 128), F32)
        high, low = split(k3[part])
        grid = z_ref[4, nz : nz + 16, 0:128]
        if part == 1:
            grid = jnp.zeros_like(grid)
        rest = jnp.concatenate([high, low, grid, jnp.zeros((48, 128), BF16)], axis=0)
        own = t3[part] + dot(later_ref[192:224, cells:], rest)
        blocks[iy, part * 24 : part * 24 + 24] = own[0:24]
    gathers = [send(6 + i, blocks.at[iy], blocks.at[iy], (ix, p)) for i, p in enumerate(peers)]

    plane_w.wait_recv()
    plane_a.wait_recv()
    for part in range(2):
        w, a = plane[0], plane[1]
        value = -(w + 0.5 * a) if part == 0 else 0.5 * w - a
        rows = jnp.concatenate([row_got[part * 32 + c * 8 : part * 32 + c * 8 + 8] for c in range(nz // 128)], axis=1)
        edge = jnp.concatenate([corner_got[part * 4 + c : part * 4 + c + 1] for c in range(nz // 128)], axis=1)
        high, low = split(jnp.concatenate([value, rows, edge, jnp.zeros((7, nz), F32)], axis=0))
        for a in range(3):
            z = dot(high, z_ref[a, 0:nz]) + dot(low, z_ref[a, 0:nz])
            zh, zl = split(z)
            rest = jnp.concatenate([zh, zl, jnp.zeros((32, nz // 2), BF16)], axis=0)
            table = first_ref[:, cells:].reshape(3, 3, nx // 2, ny // 2, 128)
            add = dot(table[0:2, :, 0].reshape(-1, 128), rest)
            one_ref[part, 0:2, :, a, 0] += add.reshape(2, 3, ny // 2, nz // 2)
            add = dot(table[2, 0:2].reshape(-1, 128), rest).reshape(2, nx // 2, ny // 2, nz // 2)
            one_ref[part, 2, 0:2, a, :, 0:8] += add[:, :, 0:8]
            add = dot(table[0:2, 0:2, 1:].reshape(-1, 128), rest).reshape(2, 2, nx // 2 - 1, ny // 2, nz // 2)
            one_ref[part, 0:2, 0:2, a, 1:, 0:8] += add[:, :, :, 0:8]

    x2.wait_recv()
    for part in range(2):
        k2[part, 0:32] = x2_got[part * 32 : part * 32 + 32]
        for e in range(2):
            lanes = slice(e * 128, e * 128 + 128)
            k2[part, 32:40, lanes] = row_got[64 + e * 16 + part * 8 : 64 + e * 16 + part * 8 + 8]
            k2[part, 40:44, lanes] = corner_got[8 + e * 8 + part * 4 : 8 + e * 8 + part * 4 + 4]
        k2[part, 44:48] = jnp.zeros((4, nz // 2), F32)
        high, low = split(k2[part])
        grid = z_ref[3, nz : nz + 16]
        if part == 1:
            grid = jnp.zeros_like(grid)
        rest = jnp.concatenate([high, low, grid, jnp.zeros((16, nz // 2), BF16)], axis=0)
        own = t2[part] + dot(later_ref[0:144, cells:], rest)
        shape = (3, 3, nx // 4, ny // 4, nz // 4)
        two_ref[part, :, :, 1] = own[:, 0:128].reshape(shape)
        two_ref[part, :, :, 2] = own[:, 128:256].reshape(shape)
        two_ref[part, :, :, 0] = pltpu.roll(own[:, 128:256], 1, 1).reshape(shape)

    for copy in gathers:
        copy.wait_recv()
    loads[6].wait()
    shape = (3, 3, 1, sy * ny // 8, nz // 8)
    for part in range(2):
        rows = jnp.concatenate([blocks[g, part * 24 : part * 24 + 24] for g in range(sy)], axis=0)
        high, low = split(rows)
        out = dot(gather_ref[...], jnp.concatenate([high, low], axis=0))
        lane = lax.broadcasted_iota(jnp.int32, out.shape, 1)
        upper = pltpu.roll(out, 64, 1)
        lower = jnp.where(lane == 0, 0.0, pltpu.roll(out, 65, 1))
        three_ref[part, :, :, 1] = out[:, 0:64].reshape(shape)
        three_ref[part, :, :, 2] = upper[:, 0:64].reshape(shape)
        three_ref[part, :, :, 0] = lower[:, 0:64].reshape(shape)

    for copy in (plane_w, plane_a, x3, x2, row, corner, *gathers):
        copy.wait_send()


def solution(mesh):
    sx, sy = mesh.shape["gx"], mesh.shape["gy"]

    def local(wave_sq, absorb):
        nx, ny, nz = wave_sq.shape
        first, later = xy_tables(nx, ny, sx, sy)
        tables = [
            jnp.asarray(t.astype(ml_dtypes.bfloat16)) for t in (first, later, z_tables(nz), gather_table(sy, ny // 8))
        ]
        first, later, depth, gather = tables
        half = nz // 2
        return pl.pallas_call(
            functools.partial(halo_kernel, sx, sy),
            out_shape=(
                jax.ShapeDtypeStruct((2, 3, 3, 3, nx // 2, ny // 2, nz // 2), F32),
                jax.ShapeDtypeStruct((2, 3, 3, 3, nx // 4, ny // 4, nz // 4), F32),
                jax.ShapeDtypeStruct((2, 3, 3, 3, nx // 8, sy * ny // 8, nz // 8), F32),
            ),
            in_specs=[pl.BlockSpec(memory_space=pl.ANY)] * 6,
            out_specs=[pl.BlockSpec(memory_space=pltpu.VMEM)] * 3,
            scratch_shapes=[
                pltpu.VMEM((nx, ny, nz), F32),
                pltpu.VMEM((nx, ny, nz), F32),
                pltpu.VMEM(first.shape[1:], BF16),
                pltpu.VMEM(later.shape[1:], BF16),
                pltpu.VMEM(depth.shape, BF16),
                pltpu.VMEM(gather.shape, BF16),
                pltpu.VMEM((2, 2, nx * ny, nz), BF16),
                pltpu.VMEM((2, ny, nz), F32),
                pltpu.VMEM((104, 128), F32),
                pltpu.VMEM((104, 128), F32),
                pltpu.VMEM((32, 128), F32),
                pltpu.VMEM((32, 128), F32),
                pltpu.VMEM((64, half), F32),
                pltpu.VMEM((64, half), F32),
                pltpu.VMEM((32, 128), F32),
                pltpu.VMEM((32, 128), F32),
                pltpu.VMEM((sy, 48, 128), F32),
                pltpu.VMEM((2, 144, half), F32),
                pltpu.VMEM((2, 32, 128), F32),
                pltpu.VMEM((2, HALO, half), F32),
                pltpu.VMEM((2, 32, 128), F32),
                pltpu.VMEM((2, nz // 128, nx, 128), F32),
                pltpu.SemaphoreType.DMA((7,)),
                pltpu.SemaphoreType.DMA((6 + sy - 1,)),
                pltpu.SemaphoreType.DMA((6 + sy - 1,)),
            ],
            compiler_params=pltpu.CompilerParams(
                collective_id=0, has_side_effects=True, vmem_limit_bytes=32 * 1024 * 1024
            ),
        )(wave_sq, absorb, first, later, depth, gather)

    return jax.shard_map(
        local,
        mesh=mesh,
        in_specs=(P("gx", "gy", None), P("gx", "gy", None)),
        out_specs=(
            P(None, None, None, None, "gx", "gy", None),
            P(None, None, None, None, "gx", "gy", None),
            P(None, None, None, None, "gx", None, None),
        ),
        check_vma=False,
    )
```

time: 209 us -> 44.6 us (0.21)
  the two profiles are of different devices: /device:TPU:7 before, /device:TPU:1 now
where the time goes in v1:
time: 44.6 us; the launch traced here: 44.2 us
  Pallas kernels  32.2 us (72%)
  local copies, waits for them, and re-layouts  11.4 us (26%)
  between operations  0.65 us (1%)
    pallas_call x1, Pallas kernels, local(): pl.pallas_call(functools.partial(halo_kernel, sx, sy), out_shape=(jax.Sha...  32.2 us
    unnamed x15, local copies, waits for them, and re-layouts  11.4 us

profile of v1, /device:TPU:1, one launch (start us, length us, event | category | flops | bytes accessed | tf_op | source)
XLA Modules:
  0.0 44.2 jit_solution(13667143362822148808)
XLA Ops:
  0.6 0.0 copy-start
  0.6 2.1 %copy-done = bf16[9,576,384]{2,1,0:T(8,128)(2,1)S(1)} copy-done((bf16[9,576,384]{2,1,0:T(8,128)(2,1)S(1)}, bf16[9,576,384]{2,1,0:T(8,128)(2,1)}, u32[]{:S(2)}) %copy-start) | copy-done | bytes 3981336
  2.8 0.0 copy-start.1
  2.8 1.6 %copy-done.1 = bf16[9,320,384]{2,1,0:T(8,128)(2,1)S(1)} copy-done((bf16[9,320,384]{2,1,0:T(8,128)(2,1)S(1)}, bf16[9,320,384]{2,1,0:T(8,128)(2,1)}, u32[]{:S(2)}) %copy-start.1) | copy-done | bytes 2211864
  4.4 0.0 copy-start.2
  4.4 1.3 %copy-done.2 = bf16[5,528,256]{2,1,0:T(8,128)(2,1)S(1)} copy-done((bf16[5,528,256]{2,1,0:T(8,128)(2,1)S(1)}, bf16[5,528,256]{2,1,0:T(8,128)(2,1)}, u32[]{:S(2)}) %copy-start.2) | copy-done | bytes 1351704
  5.7 0.0 copy-start.3
  5.7 1.0 %copy-done.3 = f32[8,32,512]{2,1,0:T(8,128)S(1)} copy-done((f32[8,32,512]{2,1,0:T(8,128)S(1)}, f32[8,32,512]{2,1,0:T(8,128)}, u32[]{:S(2)}) %copy-start.3) | copy-done | bytes 524312
  6.8 0.0 copy-start.4
  6.8 1.0 %copy-done.4 = f32[8,32,512]{2,1,0:T(8,128)S(1)} copy-done((f32[8,32,512]{2,1,0:T(8,128)S(1)}, f32[8,32,512]{2,1,0:T(8,128)}, u32[]{:S(2)}) %copy-start.4) | copy-done | bytes 524312
  7.8 0.0 copy-start.5
  7.8 0.9 %copy-done.5 = bf16[144,192]{1,0:T(8,128)(2,1)S(1)} copy-done((bf16[144,192]{1,0:T(8,128)(2,1)S(1)}, bf16[144,192]{1,0:T(8,128)(2,1)}, u32[]{:S(2)}) %copy-start.5) | copy-done | bytes 55320
  8.7 32.2 %shard_map.85 = (f32[2,3,3,3,4,16,256]{6,5,4,3,2,1,0:T(8,128)S(1)}, f32[2,3,3,3,2,8,128]{6,5,4,3,2,1,0:T(8,128)S(1)}, f32[2,3,3,3,1,16,64]{6,5,4,3,2,1,0:T(8,128)S(1)}) custom-call(f32[8,32,512]{2,1,0:T(8,128)S(1)} %copy-done.3, f32[8,32,512]{2,1,0:T(8,128)S(1)} %copy-done.4, bf16[9,576,384]{2,1,0:T(8,128)(2,1)S(1)} %copy-done, ...), custom_call_target="tpu_custom_call" | custom-call | tf_op jit(solution)/shard_map/pallas_call | solution.py:425
  40.9 1.8 %copy.12 = f32[2,3,3,3,4,16,256]{6,5,4,3,2,1,0:T(8,128)} copy(f32[2,3,3,3,4,16,256]{6,5,4,3,2,1,0:T(8,128)S(1)} %get-tuple-element.6) | data formatting | bytes 7077888
  42.7 0.8 %copy.13 = f32[2,3,3,3,2,8,128]{6,5,4,3,2,1,0:T(8,128)} copy(f32[2,3,3,3,2,8,128]{6,5,4,3,2,1,0:T(8,128)S(1)} %get-tuple-element.7) | data formatting | bytes 884736
  43.5 0.8 %copy.14 = f32[2,3,3,3,1,16,64]{6,5,4,3,2,1,0:T(8,128)} copy(f32[2,3,3,3,1,16,64]{6,5,4,3,2,1,0:T(8,128)S(1)} %get-tuple-element.8) | data formatting | bytes 442368
Async XLA Ops:
  0.6 2.1 %copy-start = (bf16[9,576,384]{2,1,0:T(8,128)(2,1)S(1)}, bf16[9,576,384]{2,1,0:T(8,128)(2,1)}, u32[]{:S(2)}) copy-start(bf16[9,576,384]{2,1,0:T(8,128)(2,1)} %constant.8.clone.first_hbm) | copy-start | bytes 11943940
  2.8 1.6 %copy-start.1 = (bf16[9,320,384]{2,1,0:T(8,128)(2,1)S(1)}, bf16[9,320,384]{2,1,0:T(8,128)(2,1)}, u32[]{:S(2)}) copy-start(bf16[9,320,384]{2,1,0:T(8,128)(2,1)} %constant.9.clone.later_hbm) | copy-start | bytes 6635524
  4.4 1.3 %copy-start.2 = (bf16[5,528,256]{2,1,0:T(8,128)(2,1)S(1)}, bf16[5,528,256]{2,1,0:T(8,128)(2,1)}, u32[]{:S(2)}) copy-start(bf16[5,528,256]{2,1,0:T(8,128)(2,1)} %constant.10.clone.z_hbm) | copy-start | bytes 4055044
  5.7 1.0 %copy-start.3 = (f32[8,32,512]{2,1,0:T(8,128)S(1)}, f32[8,32,512]{2,1,0:T(8,128)}, u32[]{:S(2)}) copy-start(f32[8,32,512]{2,1,0:T(8,128)} %w_hbm.1) | copy-start | bytes 1572868
  6.8 1.0 %copy-start.4 = (f32[8,32,512]{2,1,0:T(8,128)S(1)}, f32[8,32,512]{2,1,0:T(8,128)}, u32[]{:S(2)}) copy-start(f32[8,32,512]{2,1,0:T(8,128)} %a_hbm.1) | copy-start | bytes 1572868
  7.8 0.9 %copy-start.5 = (bf16[144,192]{1,0:T(8,128)(2,1)S(1)}, bf16[144,192]{1,0:T(8,128)(2,1)}, u32[]{:S(2)}) copy-start(bf16[144,192]{1,0:T(8,128)(2,1)} %constant.11.clone.gather_hbm) | copy-start | bytes 165892

commit v2 on v1

--- a/solution.py
+++ b/solution.py
@@ -230,7 +230,7 @@
 def halo_kernel(
     sx, sy,
     w_hbm, a_hbm, first_hbm, later_hbm, z_hbm, gather_hbm,
-    one_ref, two_ref, three_ref,
+    one_ref, t2_ref, x2_ref, three_ref,
     w_ref, a_ref, first_ref, later_ref, z_ref, gather_ref,
     mass, plane, row_send, row_got, corner_send, corner_got,
     x2_send, x2_got, x3_send, x3_got, blocks, t2, t3, k2, k3, raw,
@@ -241,6 +241,8 @@
     cells = nx * ny
     next_x, last_x = lax.rem(ix + 1, sx), lax.rem(ix + sx - 1, sx)
     next_y, last_y = lax.rem(iy + 1, sy), lax.rem(iy + sy - 1, sy)
+    from_x, to_x, from_y, to_y = ix > 0, ix < sx - 1, iy > 0, iy < sy - 1
+    from_xy, to_xy = from_x & from_y, to_x & to_y
     peers = [lax.rem(iy + step, sy) for step in range(1, sy)]
 
     place_x = jnp.where(ix == 0, FIRST, jnp.where(ix == sx - 1, LAST, MIDDLE))
@@ -263,22 +265,48 @@
     for load in loads:
         load.start()
 
+    @pl.when(jnp.logical_not(from_x))
+    def _():
+        plane[...] = jnp.zeros_like(plane)
+        x2_got[...] = jnp.zeros_like(x2_got)
+        x3_got[...] = jnp.zeros_like(x3_got)
+
+    @pl.when(jnp.logical_not(from_y))
+    def _():
+        row_got[...] = jnp.zeros_like(row_got)
+
+    @pl.when(jnp.logical_not(from_xy))
+    def _():
+        corner_got[...] = jnp.zeros_like(corner_got)
+
+    def signal(*device):
+        pl.semaphore_signal(barrier, inc=1, device_id=device, device_id_type=MESH)
+
     barrier = pltpu.get_barrier_semaphore()
-    sources = [(last_x, iy), (last_x, last_y)] + [(ix, p) for p in peers]
-    for device in sources:
-        pl.semaphore_signal(barrier, inc=1, device_id=device, device_id_type=MESH)
-    pl.semaphore_wait(barrier, len(sources))
-
-    def send(slot, src, dst, device):
-        copy = pltpu.make_async_remote_copy(
+    for p in peers:
+        signal(ix, p)
+    pl.when(from_x)(lambda: signal(last_x, iy))
+    pl.when(from_xy)(lambda: signal(last_x, last_y))
+    pl.semaphore_wait(barrier, sy - 1 + to_x.astype(jnp.int32) + to_xy.astype(jnp.int32))
+
+    def remote(slot, src, dst, device):
+        return pltpu.make_async_remote_copy(
             src_ref=src, dst_ref=dst, send_sem=send_sem.at[slot], recv_sem=got_sem.at[slot],
             device_id=device, device_id_type=MESH,
         )
-        copy.start()
-        return copy
-
-    plane_w = send(0, w_hbm.at[nx - 1], plane.at[0], (next_x, iy))
-    plane_a = send(1, a_hbm.at[nx - 1], plane.at[1], (next_x, iy))
+
+    plane_w = remote(0, w_hbm.at[nx - 1], plane.at[0], (next_x, iy))
+    plane_a = remote(1, a_hbm.at[nx - 1], plane.at[1], (next_x, iy))
+    x3 = remote(2, x3_send, x3_got, (next_x, iy))
+    x2 = remote(3, x2_send, x2_got, (next_x, iy))
+    row = remote(4, row_send, row_got, (ix, next_y))
+    corner = remote(5, corner_send, corner_got, (next_x, next_y))
+    gathers = [remote(6 + i, blocks.at[iy], blocks.at[iy], (ix, p)) for i, p in enumerate(peers)]
+
+    @pl.when(to_x)
+    def _():
+        plane_w.start()
+        plane_a.start()
 
     loads[0].wait()
     loads[1].wait()
@@ -313,10 +341,13 @@
             row_send[part * 32 + c * 8 : part * 32 + c * 8 + 8] = raw[part, c]
             corner_send[part * 4 + c : part * 4 + c + 1] = raw[part, c, nx - 1 : nx]
 
-    x3 = send(2, x3_send, x3_got, (next_x, iy))
-    x2 = send(3, x2_send, x2_got, (next_x, iy))
-    row = send(4, row_send, row_got, (ix, next_y))
-    corner = send(5, corner_send, corner_got, (next_x, next_y))
+    @pl.when(to_x)
+    def _():
+        x3.start()
+        x2.start()
+
+    pl.when(to_y)(row.start)
+    pl.when(to_xy)(corner.start)
 
     loads[4].wait()
     loads[5].wait()
@@ -336,9 +367,9 @@
 
     lax.fori_loop(0, 6, own_level_one, 0)
 
-    row.wait_recv()
-    corner.wait_recv()
-    x3.wait_recv()
+    pl.when(from_y)(row.wait_recv)
+    pl.when(from_xy)(corner.wait_recv)
+    pl.when(from_x)(x3.wait_recv)
     for part in range(2):
         k3[part, 0:16] = x3_got[part * 16 : part * 16 + 16]
         k3[part, 16:20] = row_got[96 + part * 4 : 96 + part * 4 + 4]
@@ -351,10 +382,29 @@
         rest = jnp.concatenate([high, low, grid, jnp.zeros((48, 128), BF16)], axis=0)
         own = t3[part] + dot(later_ref[192:224, cells:], rest)
         blocks[iy, part * 24 : part * 24 + 24] = own[0:24]
-    gathers = [send(6 + i, blocks.at[iy], blocks.at[iy], (ix, p)) for i, p in enumerate(peers)]
-
-    plane_w.wait_recv()
-    plane_a.wait_recv()
+    for copy in gathers:
+        copy.start()
+
+    for part in range(2):
+        k2[part, 0:32] = jnp.zeros((32, nz // 2), F32)
+        for e in range(2):
+            lanes = slice(e * 128, e * 128 + 128)
+            k2[part, 32:40, lanes] = row_got[64 + e * 16 + part * 8 : 64 + e * 16 + part * 8 + 8]
+            k2[part, 40:44, lanes] = corner_got[8 + e * 8 + part * 4 : 8 + e * 8 + part * 4 + 4]
+        k2[part, 44:48] = jnp.zeros((4, nz // 2), F32)
+        high, low = split(k2[part])
+        grid = z_ref[3, nz : nz + 16]
+        if part == 1:
+            grid = jnp.zeros_like(grid)
+        rest = jnp.concatenate([high, low, grid, jnp.zeros((16, nz // 2), BF16)], axis=0)
+        t2_ref[part] = t2[part] + dot(later_ref[0:144, cells:], rest)
+
+
+    @pl.when(from_x)
+    def _():
+        plane_w.wait_recv()
+        plane_a.wait_recv()
+
     for part in range(2):
         w, a = plane[0], plane[1]
         value = -(w + 0.5 * a) if part == 0 else 0.5 * w - a
@@ -373,25 +423,6 @@
             add = dot(table[0:2, 0:2, 1:].reshape(-1, 128), rest).reshape(2, 2, nx // 2 - 1, ny // 2, nz // 2)
             one_ref[part, 0:2, 0:2, a, 1:, 0:8] += add[:, :, :, 0:8]
 
-    x2.wait_recv()
-    for part in range(2):
-        k2[part, 0:32] = x2_got[part * 32 : part * 32 + 32]
-        for e in range(2):
-            lanes = slice(e * 128, e * 128 + 128)
-            k2[part, 32:40, lanes] = row_got[64 + e * 16 + part * 8 : 64 + e * 16 + part * 8 + 8]
-            k2[part, 40:44, lanes] = corner_got[8 + e * 8 + part * 4 : 8 + e * 8 + part * 4 + 4]
-        k2[part, 44:48] = jnp.zeros((4, nz // 2), F32)
-        high, low = split(k2[part])
-        grid = z_ref[3, nz : nz + 16]
-        if part == 1:
-            grid = jnp.zeros_like(grid)
-        rest = jnp.concatenate([high, low, grid, jnp.zeros((16, nz // 2), BF16)], axis=0)
-        own = t2[part] + dot(later_ref[0:144, cells:], rest)
-        shape = (3, 3, nx // 4, ny // 4, nz // 4)
-        two_ref[part, :, :, 1] = own[:, 0:128].reshape(shape)
-        two_ref[part, :, :, 2] = own[:, 128:256].reshape(shape)
-        two_ref[part, :, :, 0] = pltpu.roll(own[:, 128:256], 1, 1).reshape(shape)
-
     for copy in gathers:
         copy.wait_recv()
     loads[6].wait()
@@ -407,8 +438,52 @@
         three_ref[part, :, :, 2] = upper[:, 0:64].reshape(shape)
         three_ref[part, :, :, 0] = lower[:, 0:64].reshape(shape)
 
-    for copy in (plane_w, plane_a, x3, x2, row, corner, *gathers):
+    pl.when(from_x)(x2.wait_recv)
+    x2_ref[...] = x2_got[...]
+
+    for copy in gathers:
         copy.wait_send()
+    pl.when(to_y)(row.wait_send)
+    pl.when(to_xy)(corner.wait_send)
+
+    @pl.when(to_x)
+    def _():
+        for copy in (plane_w, plane_a, x3, x2):
+            copy.wait_send()
+
+
+def result_kernel(one_ref, t2_ref, x2_ref, three_ref, one_hbm, two_hbm, three_hbm, two, sem):
+    ones = [
+        pltpu.make_async_copy(one_ref.at[part, a], one_hbm.at[part, a], sem.at[3 * part + a])
+        for part in range(2)
+        for a in range(3)
+    ]
+    three = pltpu.make_async_copy(three_ref, three_hbm, sem.at[6])
+    three.start()
+    for copy in ones:
+        copy.start()
+    _, _, _, _, m, n, depth = two.shape
+    for part in range(2):
+        whole = t2_ref[part].reshape(3, 3, m, n, 2 * depth)
+        for a in range(3):
+            for b in range(3):
+                for x in range(m):
+                    value = whole[a, b, x]
+                    if x == 0 and a < 2:
+                        base = part * 32 + a * 2 * n
+                        if b > 0:
+                            value = value + x2_ref[base + (b - 1) * n : base + b * n]
+                        else:
+                            above = pltpu.roll(x2_ref[base + n : base + 2 * n], 1, 0)
+                            line = lax.broadcasted_iota(jnp.int32, above.shape, 0)
+                            value = value + jnp.where(line == 0, 0.0, above)
+                    two[part, a, b, 1, x] = value[:, 0:depth]
+                    two[part, a, b, 2, x] = value[:, depth:]
+                    two[part, a, b, 0, x] = pltpu.roll(value[:, depth:], 1, 1)
+    copy = pltpu.make_async_copy(two, two_hbm, sem.at[7])
+    copy.start()
+    for done in (three, *ones, copy):
+        done.wait()
 
 
 def solution(mesh):
@@ -422,15 +497,19 @@
         ]
         first, later, depth, gather = tables
         half = nz // 2
-        return pl.pallas_call(
+        level_one = jax.ShapeDtypeStruct((2, 3, 3, 3, nx // 2, ny // 2, nz // 2), F32)
+        level_two = jax.ShapeDtypeStruct((2, 3, 3, 3, nx // 4, ny // 4, nz // 4), F32)
+        level_three = jax.ShapeDtypeStruct((2, 3, 3, 3, nx // 8, sy * ny // 8, nz // 8), F32)
+        parts = pl.pallas_call(
             functools.partial(halo_kernel, sx, sy),
             out_shape=(
-                jax.ShapeDtypeStruct((2, 3, 3, 3, nx // 2, ny // 2, nz // 2), F32),
-                jax.ShapeDtypeStruct((2, 3, 3, 3, nx // 4, ny // 4, nz // 4), F32),
-                jax.ShapeDtypeStruct((2, 3, 3, 3, nx // 8, sy * ny // 8, nz // 8), F32),
+                level_one,
+                jax.ShapeDtypeStruct((2, 144, half), F32),
+                jax.ShapeDtypeStruct((64, half), F32),
+                level_three,
             ),
-            in_specs=[pl.BlockSpec(memory_space=pl.ANY)] * 6,
-            out_specs=[pl.BlockSpec(memory_space=pltpu.VMEM)] * 3,
+            in_specs=[pl.BlockSpec(memory_space=pltpu.HBM)] * 6,
+            out_specs=[pl.BlockSpec(memory_space=pltpu.VMEM)] * 4,
             scratch_shapes=[
                 pltpu.VMEM((nx, ny, nz), F32),
                 pltpu.VMEM((nx, ny, nz), F32),
@@ -461,7 +540,15 @@
             compiler_params=pltpu.CompilerParams(
                 collective_id=0, has_side_effects=True, vmem_limit_bytes=32 * 1024 * 1024
             ),
-        )(wave_sq, absorb, first, later, depth, gather)
+        )(*[pltpu.with_memory_space_constraint(v, pltpu.HBM) for v in (wave_sq, absorb, first, later, depth, gather)])
+        return pl.pallas_call(
+            result_kernel,
+            out_shape=(level_one, level_two, level_three),
+            in_specs=[pl.BlockSpec(memory_space=pltpu.VMEM)] * 4,
+            out_specs=[pl.BlockSpec(memory_space=pltpu.HBM)] * 3,
+            scratch_shapes=[pltpu.VMEM(level_two.shape, F32), pltpu.SemaphoreType.DMA((8,))],
+            compiler_params=pltpu.CompilerParams(vmem_limit_bytes=16 * 1024 * 1024),
+        )(*parts)
 
     return jax.shard_map(
         local,

time: 44.6 us -> 31.5 us (0.71)
  the two profiles are of different devices: /device:TPU:1 before, /device:TPU:7 now
where the time goes in v2:
time: 31.5 us; the launch traced here: 31.4 us
  Pallas kernels  30.8 us (98%)
  between operations  0.64 us (2%)
    pallas_call x1, Pallas kernels, local(): pl.pallas_call(functools.partial(halo_kernel, sx, sy), out_shape=(level_o...  28.6 us
    pallas_call x1, Pallas kernels, local(): pl.pallas_call(result_kernel, out_shape=(level_one, level_two, level_thre...  2.14 us

profile of v2, /device:TPU:7, one launch (start us, length us, event | category | flops | bytes accessed | tf_op | source)
XLA Modules:
  0.0 31.4 jit_solution(15634880483308955518)
XLA Ops:
  0.6 28.6 %shard_map.85 = (f32[2,3,3,3,4,16,256]{6,5,4,3,2,1,0:T(8,128)S(1)}, f32[2,144,256]{2,1,0:T(8,128)S(1)}, f32[64,256]{1,0:T(8,128)S(1)}, f32[2,3,3,3,1,16,64]{6,5,4,3,2,1,0:T(8,128)S(1)}) custom-call(f32[8,32,512]{2,1,0:T(8,128)} %w_hbm.1, f32[8,32,512]{2,1,0:T(8,128)} %a_hbm.1, bf16[9,576,384]{2,1,0:T(8,128)(2,1)} %constant.8.clone.first_hbm, ...), custom_call_target="tpu_custom_call" | custom-call | tf_op jit(solution)/shard_map/pallas_call | solution.py:503
  29.3 2.1 %shard_map.86 = (f32[2,3,3,3,4,16,256]{6,5,4,3,2,1,0:T(8,128)}, f32[2,3,3,3,2,8,128]{6,5,4,3,2,1,0:T(8,128)}, f32[2,3,3,3,1,16,64]{6,5,4,3,2,1,0:T(8,128)}) custom-call(f32[2,3,3,3,4,16,256]{6,5,4,3,2,1,0:T(8,128)S(1)} %get-tuple-element.7.one_ref, f32[2,144,256]{2,1,0:T(8,128)S(1)} %get-tuple-element.8.t2_ref, f32[64,256]{1,0:T(8,128)S(1)} %get-tuple-element.9.x2_ref, ...), custom_call_target="tpu_custom_call" | custom-call | tf_op jit(solution)/shard_map/pallas_call | solution.py:544

commit v3 on v2

--- a/solution.py
+++ b/solution.py
@@ -211,6 +211,7 @@
 
 
 HALO = 48
+TURNS = 4
 
 
 def split(value):
@@ -230,10 +231,10 @@
 def halo_kernel(
     sx, sy,
     w_hbm, a_hbm, first_hbm, later_hbm, z_hbm, gather_hbm,
-    one_ref, t2_ref, x2_ref, three_ref,
-    w_ref, a_ref, first_ref, later_ref, z_ref, gather_ref,
-    mass, plane, row_send, row_got, corner_send, corner_got,
-    x2_send, x2_got, x3_send, x3_got, blocks, t2, t3, k2, k3, raw,
+    one_ref, t2_ref, x2_got, blocks, plane, edge, z_ref, head_ref, gather_ref,
+    w_ref, a_ref, first_ref, later_ref, later_z_ref,
+    mass, row_send, row_got, corner_send, corner_got,
+    x2_send, x3_send, x3_got, t2, t3, k2, k3, raw, through,
     load_sem, send_sem, got_sem,
 ):
     ix, iy = lax.axis_index("gx"), lax.axis_index("gy")
@@ -243,6 +244,12 @@
     next_y, last_y = lax.rem(iy + 1, sy), lax.rem(iy + sy - 1, sy)
     from_x, to_x, from_y, to_y = ix > 0, ix < sx - 1, iy > 0, iy < sy - 1
     from_xy, to_xy = from_x & from_y, to_x & to_y
+    turn = sx // TURNS
+    turning = sx == TURNS * 32
+    at = lax.rem(ix, turn)
+    leads = to_x & (at == turn - 1) & turning
+    helps = (ix < sx - turn) & (at == 3) & turning
+    waits = from_x & (at == 0) & turning
     peers = [lax.rem(iy + step, sy) for step in range(1, sy)]
 
     place_x = jnp.where(ix == 0, FIRST, jnp.where(ix == sx - 1, LAST, MIDDLE))
@@ -255,14 +262,14 @@
                 (w_hbm, w_ref),
                 (a_hbm, a_ref),
                 (later_hbm.at[place], later_ref),
-                (z_hbm.at[pl.ds(3, 2)], z_ref.at[pl.ds(3, 2)]),
-                (z_hbm.at[pl.ds(0, 3)], z_ref.at[pl.ds(0, 3)]),
+                (z_hbm.at[pl.ds(3, 2)], later_z_ref),
+                (z_hbm.at[pl.ds(0, 3)], z_ref),
                 (first_hbm.at[place], first_ref),
                 (gather_hbm, gather_ref),
             )
         )
     ]
-    for load in loads:
+    for load in loads[:4]:
         load.start()
 
     @pl.when(jnp.logical_not(from_x))
@@ -287,11 +294,15 @@
         signal(ix, p)
     pl.when(from_x)(lambda: signal(last_x, iy))
     pl.when(from_xy)(lambda: signal(last_x, last_y))
-    pl.semaphore_wait(barrier, sy - 1 + to_x.astype(jnp.int32) + to_xy.astype(jnp.int32))
-
-    def remote(slot, src, dst, device):
+    pl.when(waits)(lambda: signal(ix - turn + 3, iy))
+    pl.when(helps)(lambda: signal(ix + turn - 4, iy))
+    sends_to = [flag.astype(jnp.int32) for flag in (to_x, to_xy, leads, helps)]
+    pl.semaphore_wait(barrier, sy - 1 + sum(sends_to))
+
+    def remote(slot, src, dst, device, got=None):
+        got = slot if got is None else got
         return pltpu.make_async_remote_copy(
-            src_ref=src, dst_ref=dst, send_sem=send_sem.at[slot], recv_sem=got_sem.at[slot],
+            src_ref=src, dst_ref=dst, send_sem=send_sem.at[slot], recv_sem=got_sem.at[got],
             device_id=device, device_id_type=MESH,
         )
 
@@ -303,10 +314,13 @@
     corner = remote(5, corner_send, corner_got, (next_x, next_y))
     gathers = [remote(6 + i, blocks.at[iy], blocks.at[iy], (ix, p)) for i, p in enumerate(peers)]
 
-    @pl.when(to_x)
-    def _():
-        plane_w.start()
-        plane_a.start()
+    lead = remote(5 + sy, a_hbm.at[nx - 1], through, (jnp.maximum(ix - turn + 4, 0), iy))
+    follow = remote(6 + sy, through, plane.at[1], (jnp.minimum(ix + turn - 3, sx - 1), iy), got=1)
+
+    pl.when(to_x)(plane_w.start)
+    pl.when(leads)(lead.start)
+    for load in loads[4:]:
+        load.start()
 
     loads[0].wait()
     loads[1].wait()
@@ -325,9 +339,9 @@
         table = later_ref[:, 0:cells]
         rows = dot(table, mass[part, 0]) + dot(table, mass[part, 1])
         high, low = split(rows[0:192])
-        two = dot(high, z_ref[3, 0:nz]) + dot(low, z_ref[3, 0:nz])
+        two = dot(high, later_z_ref[0, 0:nz]) + dot(low, later_z_ref[0, 0:nz])
         high, low = split(rows[192:256] + rows[256:320])
-        three = dot(high, z_ref[4, 0:nz, 0:128]) + dot(low, z_ref[4, 0:nz, 0:128])
+        three = dot(high, later_z_ref[1, 0:nz, 0:128]) + dot(low, later_z_ref[1, 0:nz, 0:128])
         t2[part] = two[0:144]
         t3[part] = three[0:32]
         x3_send[part * 16 : part * 16 + 16] = three[32:48]
@@ -341,13 +355,12 @@
             row_send[part * 32 + c * 8 : part * 32 + c * 8 + 8] = raw[part, c]
             corner_send[part * 4 + c : part * 4 + c + 1] = raw[part, c, nx - 1 : nx]
 
-    @pl.when(to_x)
-    def _():
-        x3.start()
-        x2.start()
-
+    pl.when(to_x)(x3.start)
+    pl.when(to_xy)(corner.start)
     pl.when(to_y)(row.start)
-    pl.when(to_xy)(corner.start)
+
+    pl.when(to_x & jnp.logical_not(leads))(plane_a.start)
+    pl.when(to_x)(x2.start)
 
     loads[4].wait()
     loads[5].wait()
@@ -376,7 +389,7 @@
         k3[part, 20:24] = corner_got[24 + part * 4 : 24 + part * 4 + 4]
         k3[part, 24:32] = jnp.zeros((8, 128), F32)
         high, low = split(k3[part])
-        grid = z_ref[4, nz : nz + 16, 0:128]
+        grid = later_z_ref[1, nz : nz + 16, 0:128]
         if part == 1:
             grid = jnp.zeros_like(grid)
         rest = jnp.concatenate([high, low, grid, jnp.zeros((48, 128), BF16)], axis=0)
@@ -393,75 +406,98 @@
             k2[part, 40:44, lanes] = corner_got[8 + e * 8 + part * 4 : 8 + e * 8 + part * 4 + 4]
         k2[part, 44:48] = jnp.zeros((4, nz // 2), F32)
         high, low = split(k2[part])
-        grid = z_ref[3, nz : nz + 16]
+        grid = later_z_ref[0, nz : nz + 16]
         if part == 1:
             grid = jnp.zeros_like(grid)
         rest = jnp.concatenate([high, low, grid, jnp.zeros((16, nz // 2), BF16)], axis=0)
         t2_ref[part] = t2[part] + dot(later_ref[0:144, cells:], rest)
 
+    for part in range(2):
+        rows = jnp.concatenate([row_got[part * 32 + c * 8 : part * 32 + c * 8 + 8] for c in range(nz // 128)], axis=1)
+        last = jnp.concatenate([corner_got[part * 4 + c : part * 4 + c + 1] for c in range(nz // 128)], axis=1)
+        edge[part] = jnp.concatenate([rows, last, jnp.zeros((7, nz), F32)], axis=0)
+    high, low = split(edge[...].reshape(32, nz))
+    both = jnp.concatenate([high, low], axis=0)
+    gap = jnp.zeros((32, nz // 2), BF16)
+    table = first_ref[:, cells:].reshape(3, 3, nx // 2, ny // 2, 128)
+    head_ref[...] = table[0:2, :, 0].reshape(-1, 128)
+    for a in range(3):
+        z = dot(both, z_ref[a, 0:nz])
+        zh, zl = split(z[0:32] + z[32:64])
+        for part in range(2):
+            own = slice(part * 16, part * 16 + 16)
+            rest = jnp.concatenate([gap, zh[own], gap, zl[own], gap], axis=0)
+            add = dot(table[2, 0:2].reshape(-1, 128), rest).reshape(2, nx // 2, ny // 2, nz // 2)
+            one_ref[part, 2, 0:2, a, :, 0:8] += add[:, :, 0:8]
+            add = dot(table[0:2, 0:2, 1:].reshape(-1, 128), rest).reshape(2, 2, nx // 2 - 1, ny // 2, nz // 2)
+            one_ref[part, 0:2, 0:2, a, 1:, 0:8] += add[:, :, :, 0:8]
+
+    @pl.when(helps)
+    def _():
+        lead.wait_recv()
+        follow.start()
 
     @pl.when(from_x)
     def _():
         plane_w.wait_recv()
         plane_a.wait_recv()
-
-    for part in range(2):
-        w, a = plane[0], plane[1]
-        value = -(w + 0.5 * a) if part == 0 else 0.5 * w - a
-        rows = jnp.concatenate([row_got[part * 32 + c * 8 : part * 32 + c * 8 + 8] for c in range(nz // 128)], axis=1)
-        edge = jnp.concatenate([corner_got[part * 4 + c : part * 4 + c + 1] for c in range(nz // 128)], axis=1)
-        high, low = split(jnp.concatenate([value, rows, edge, jnp.zeros((7, nz), F32)], axis=0))
-        for a in range(3):
-            z = dot(high, z_ref[a, 0:nz]) + dot(low, z_ref[a, 0:nz])
-            zh, zl = split(z)
-            rest = jnp.concatenate([zh, zl, jnp.zeros((32, nz // 2), BF16)], axis=0)
-            table = first_ref[:, cells:].reshape(3, 3, nx // 2, ny // 2, 128)
-            add = dot(table[0:2, :, 0].reshape(-1, 128), rest)
-            one_ref[part, 0:2, :, a, 0] += add.reshape(2, 3, ny // 2, nz // 2)
-            add = dot(table[2, 0:2].reshape(-1, 128), rest).reshape(2, nx // 2, ny // 2, nz // 2)
-            one_ref[part, 2, 0:2, a, :, 0:8] += add[:, :, 0:8]
-            add = dot(table[0:2, 0:2, 1:].reshape(-1, 128), rest).reshape(2, 2, nx // 2 - 1, ny // 2, nz // 2)
-            one_ref[part, 0:2, 0:2, a, 1:, 0:8] += add[:, :, :, 0:8]
-
+        x2.wait_recv()
+
+    loads[6].wait()
     for copy in gathers:
         copy.wait_recv()
-    loads[6].wait()
-    shape = (3, 3, 1, sy * ny // 8, nz // 8)
-    for part in range(2):
-        rows = jnp.concatenate([blocks[g, part * 24 : part * 24 + 24] for g in range(sy)], axis=0)
-        high, low = split(rows)
-        out = dot(gather_ref[...], jnp.concatenate([high, low], axis=0))
-        lane = lax.broadcasted_iota(jnp.int32, out.shape, 1)
-        upper = pltpu.roll(out, 64, 1)
-        lower = jnp.where(lane == 0, 0.0, pltpu.roll(out, 65, 1))
-        three_ref[part, :, :, 1] = out[:, 0:64].reshape(shape)
-        three_ref[part, :, :, 2] = upper[:, 0:64].reshape(shape)
-        three_ref[part, :, :, 0] = lower[:, 0:64].reshape(shape)
-
-    pl.when(from_x)(x2.wait_recv)
-    x2_ref[...] = x2_got[...]
-
     for copy in gathers:
         copy.wait_send()
     pl.when(to_y)(row.wait_send)
     pl.when(to_xy)(corner.wait_send)
 
+    pl.when(to_x & jnp.logical_not(leads))(plane_a.wait_send)
+    pl.when(leads)(lead.wait_send)
+    pl.when(helps)(follow.wait_send)
+
     @pl.when(to_x)
     def _():
-        for copy in (plane_w, plane_a, x3, x2):
+        for copy in (plane_w, x3, x2):
             copy.wait_send()
 
 
-def result_kernel(one_ref, t2_ref, x2_ref, three_ref, one_hbm, two_hbm, three_hbm, two, sem):
-    ones = [
-        pltpu.make_async_copy(one_ref.at[part, a], one_hbm.at[part, a], sem.at[3 * part + a])
-        for part in range(2)
-        for a in range(3)
-    ]
-    three = pltpu.make_async_copy(three_ref, three_hbm, sem.at[6])
-    three.start()
-    for copy in ones:
+def result_kernel(
+    one_ref, t2_ref, x2_ref, blocks, plane, edge, z_ref, head_ref, gather_ref,
+    one_hbm, two_hbm, three_hbm, first, two, three, sem,
+):
+    nz = plane.shape[2]
+    count = one_ref.shape[4]
+    copies = [pltpu.make_async_copy(one_ref.at[part, 2], one_hbm.at[part, 2], sem.at[part]) for part in range(2)]
+    rest = pl.ds(1, count - 1)
+    for part in range(2):
+        for a in range(2):
+            slot = sem.at[2 + 2 * part + a]
+            copies.append(
+                pltpu.make_async_copy(one_ref.at[part, a, :, :, rest], one_hbm.at[part, a, :, :, rest], slot)
+            )
+    for copy in copies:
         copy.start()
+
+    w, a = plane[0], plane[1]
+    value = jnp.concatenate([-(w + 0.5 * a), edge[0], 0.5 * w - a, edge[1]], axis=0)
+    high, low = split(value)
+    both = jnp.concatenate([high, low], axis=0)
+    half = 2 * HALO
+    for a in range(3):
+        z = dot(both, z_ref[a, 0:nz])
+        zh, zl = split(z[0:half] + z[half:])
+        for part in range(2):
+            own = slice(part * HALO, part * HALO + HALO)
+            rest = jnp.concatenate([zh[own], zl[own], jnp.zeros((32, nz // 2), BF16)], axis=0)
+            add = dot(head_ref[...], rest)
+            first[part, :, :, a] = one_ref[part, 0:2, :, a, 0] + add.reshape(2, 3, -1, nz // 2)
+    for part in range(2):
+        for a in range(2):
+            slot = sem.at[6 + 2 * part + a]
+            copy = pltpu.make_async_copy(first.at[part, a], one_hbm.at[part, a, :, :, 0], slot)
+            copy.start()
+            copies.append(copy)
+
     _, _, _, _, m, n, depth = two.shape
     for part in range(2):
         whole = t2_ref[part].reshape(3, 3, m, n, 2 * depth)
@@ -480,10 +516,24 @@
                     two[part, a, b, 1, x] = value[:, 0:depth]
                     two[part, a, b, 2, x] = value[:, depth:]
                     two[part, a, b, 0, x] = pltpu.roll(value[:, depth:], 1, 1)
-    copy = pltpu.make_async_copy(two, two_hbm, sem.at[7])
-    copy.start()
-    for done in (three, *ones, copy):
-        done.wait()
+    copies.append(pltpu.make_async_copy(two, two_hbm, sem.at[10]))
+    copies[-1].start()
+
+    shape = three.shape[1:3] + three.shape[4:]
+    for part in range(2):
+        rows = jnp.concatenate([blocks[g, part * 24 : part * 24 + 24] for g in range(blocks.shape[0])], axis=0)
+        high, low = split(rows)
+        out = dot(gather_ref[...], jnp.concatenate([high, low], axis=0))
+        lane = lax.broadcasted_iota(jnp.int32, out.shape, 1)
+        upper = pltpu.roll(out, 64, 1)
+        lower = jnp.where(lane == 0, 0.0, pltpu.roll(out, 65, 1))
+        three[part, :, :, 1] = out[:, 0:64].reshape(shape)
+        three[part, :, :, 2] = upper[:, 0:64].reshape(shape)
+        three[part, :, :, 0] = lower[:, 0:64].reshape(shape)
+    copies.append(pltpu.make_async_copy(three, three_hbm, sem.at[11]))
+    copies[-1].start()
+    for copy in copies:
+        copy.wait()
 
 
 def solution(mesh):
@@ -506,36 +556,38 @@
                 level_one,
                 jax.ShapeDtypeStruct((2, 144, half), F32),
                 jax.ShapeDtypeStruct((64, half), F32),
-                level_three,
+                jax.ShapeDtypeStruct((sy, 48, 128), F32),
+                jax.ShapeDtypeStruct((2, ny, nz), F32),
+                jax.ShapeDtypeStruct((2, 16, nz), F32),
+                jax.ShapeDtypeStruct((3, *depth.shape[1:]), BF16),
+                jax.ShapeDtypeStruct((3 * ny, 128), BF16),
+                jax.ShapeDtypeStruct(gather.shape, BF16),
             ),
             in_specs=[pl.BlockSpec(memory_space=pltpu.HBM)] * 6,
-            out_specs=[pl.BlockSpec(memory_space=pltpu.VMEM)] * 4,
+            out_specs=[pl.BlockSpec(memory_space=pltpu.VMEM)] * 9,
             scratch_shapes=[
                 pltpu.VMEM((nx, ny, nz), F32),
                 pltpu.VMEM((nx, ny, nz), F32),
                 pltpu.VMEM(first.shape[1:], BF16),
                 pltpu.VMEM(later.shape[1:], BF16),
-                pltpu.VMEM(depth.shape, BF16),
-                pltpu.VMEM(gather.shape, BF16),
+                pltpu.VMEM((2, *depth.shape[1:]), BF16),
                 pltpu.VMEM((2, 2, nx * ny, nz), BF16),
-                pltpu.VMEM((2, ny, nz), F32),
                 pltpu.VMEM((104, 128), F32),
                 pltpu.VMEM((104, 128), F32),
                 pltpu.VMEM((32, 128), F32),
                 pltpu.VMEM((32, 128), F32),
                 pltpu.VMEM((64, half), F32),
-                pltpu.VMEM((64, half), F32),
                 pltpu.VMEM((32, 128), F32),
                 pltpu.VMEM((32, 128), F32),
-                pltpu.VMEM((sy, 48, 128), F32),
                 pltpu.VMEM((2, 144, half), F32),
                 pltpu.VMEM((2, 32, 128), F32),
                 pltpu.VMEM((2, HALO, half), F32),
                 pltpu.VMEM((2, 32, 128), F32),
                 pltpu.VMEM((2, nz // 128, nx, 128), F32),
+                pltpu.VMEM((ny, nz), F32),
                 pltpu.SemaphoreType.DMA((7,)),
-                pltpu.SemaphoreType.DMA((6 + sy - 1,)),
-                pltpu.SemaphoreType.DMA((6 + sy - 1,)),
+                pltpu.SemaphoreType.DMA((7 + sy,)),
+                pltpu.SemaphoreType.DMA((7 + sy,)),
             ],
             compiler_params=pltpu.CompilerParams(
                 collective_id=0, has_side_effects=True, vmem_limit_bytes=32 * 1024 * 1024
@@ -544,9 +596,14 @@
         return pl.pallas_call(
             result_kernel,
             out_shape=(level_one, level_two, level_three),
-            in_specs=[pl.BlockSpec(memory_space=pltpu.VMEM)] * 4,
+            in_specs=[pl.BlockSpec(memory_space=pltpu.VMEM)] * 9,
             out_specs=[pl.BlockSpec(memory_space=pltpu.HBM)] * 3,
-            scratch_shapes=[pltpu.VMEM(level_two.shape, F32), pltpu.SemaphoreType.DMA((8,))],
+            scratch_shapes=[
+                pltpu.VMEM((2, 2, 3, 3, ny // 2, half), F32),
+                pltpu.VMEM(level_two.shape, F32),
+                pltpu.VMEM(level_three.shape, F32),
+                pltpu.SemaphoreType.DMA((12,)),
+            ],
             compiler_params=pltpu.CompilerParams(vmem_limit_bytes=16 * 1024 * 1024),
         )(*parts)
 

time: 31.5 us -> 28.3 us (0.90)
  Pallas kernels: 30.8 us -> 27.6 us
    pallas_call x1, Pallas kernels: 28.6 us -> 25.1 us  [local(): pl.pallas_call(functools.partial(halo_kernel, sx, sy), out_shape=(level_o...]
    pallas_call x1, Pallas kernels: 2.14 us -> 2.49 us  [local(): pl.pallas_call(result_kernel, out_shape=(level_one, level_two, level_thre...]
where the time goes in v3:
time: 28.3 us; the launch traced here: 28.2 us
  Pallas kernels  27.6 us (98%)
  between operations  0.64 us (2%)
    pallas_call x1, Pallas kernels, local(): pl.pallas_call(functools.partial(halo_kernel, sx, sy), out_shape=(level_o...  25.1 us
    pallas_call x1, Pallas kernels, local(): pl.pallas_call(result_kernel, out_shape=(level_one, level_two, level_thre...  2.49 us

profile of v3, /device:TPU:7, one launch (start us, length us, event | category | flops | bytes accessed | tf_op | source)
XLA Modules:
  0.0 28.2 jit_solution(11888689711438956130)
XLA Ops:
  0.6 25.1 %shard_map.85 = (f32[2,3,3,3,4,16,256]{6,5,4,3,2,1,0:T(8,128)S(1)}, f32[2,144,256]{2,1,0:T(8,128)S(1)}, f32[64,256]{1,0:T(8,128)S(1)}, f32[4,48,128]{2,1,0:T(8,1...) custom-call(f32[8,32,512]{2,1,0:T(8,128)} %w_hbm.1, ...), custom_call_target="tpu_custom_call" | custom-call | tf_op jit(solution)/shard_map/pallas_call | solution.py:553
  25.7 2.5 %shard_map.86 = (f32[2,3,3,3,4,16,256]{6,5,4,3,2,1,0:T(8,128)}, f32[2,3,3,3,2,8,128]{6,5,4,3,2,1,0:T(8,128)}, f32[2,3,3,3,1,16,64]{6,5,4,3,2,1,0:T(8,128)}) custom-call(f32[2,3,3,3,4,16,256]{6,5,4,3,2,1,0:T(8,128)S(1)} %get-tuple-element.12.one_ref, f32[2,144,256]{2,1,0:T(8,128)S(1)} %get-tuple-element.13.t2_ref, f32[64,256]{1,0:T(8,128)S(1)} %get-tuple-element.14.x2_ref, ...), custom_call_target="tpu_custom_call" | custom-call | tf_op jit(solution)/shard_map/pallas_call | solution.py:596

commit v4 on v3

--- a/solution.py
+++ b/solution.py
@@ -212,6 +212,7 @@
 
 HALO = 48
 TURNS = 4
+RELAYS = (7, 3)
 
 
 def split(value):
@@ -248,8 +249,10 @@
     turning = sx == TURNS * 32
     at = lax.rem(ix, turn)
     leads = to_x & (at == turn - 1) & turning
-    helps = (ix < sx - turn) & (at == 3) & turning
+    helps = [(ix < sx - turn) & (at == place) & turning for place in RELAYS]
     waits = from_x & (at == 0) & turning
+    upper = iy >= sy // 2
+    yields = to_x & turning & (((at == turn - 2) & upper) | ((at == turn - 4) & jnp.logical_not(upper)))
     peers = [lax.rem(iy + step, sy) for step in range(1, sy)]
 
     place_x = jnp.where(ix == 0, FIRST, jnp.where(ix == sx - 1, LAST, MIDDLE))
@@ -294,9 +297,10 @@
         signal(ix, p)
     pl.when(from_x)(lambda: signal(last_x, iy))
     pl.when(from_xy)(lambda: signal(last_x, last_y))
-    pl.when(waits)(lambda: signal(ix - turn + 3, iy))
-    pl.when(helps)(lambda: signal(ix + turn - 4, iy))
-    sends_to = [flag.astype(jnp.int32) for flag in (to_x, to_xy, leads, helps)]
+    for i, place in enumerate(RELAYS):
+        pl.when(waits)(lambda place=place: signal(ix - turn + place, iy))
+        pl.when(helps[i])(lambda place=place: signal(ix + turn - 1 - place, iy))
+    sends_to = [flag.astype(jnp.int32) for flag in (to_x, to_xy, leads, leads, *helps)]
     pl.semaphore_wait(barrier, sy - 1 + sum(sends_to))
 
     def remote(slot, src, dst, device, got=None):
@@ -314,11 +318,21 @@
     corner = remote(5, corner_send, corner_got, (next_x, next_y))
     gathers = [remote(6 + i, blocks.at[iy], blocks.at[iy], (ix, p)) for i, p in enumerate(peers)]
 
-    lead = remote(5 + sy, a_hbm.at[nx - 1], through, (jnp.maximum(ix - turn + 4, 0), iy))
-    follow = remote(6 + sy, through, plane.at[1], (jnp.minimum(ix + turn - 3, sx - 1), iy), got=1)
-
-    pl.when(to_x)(plane_w.start)
-    pl.when(leads)(lead.start)
+    leading, follows = [], []
+    for i, place in enumerate(RELAYS):
+        source = (w_hbm, a_hbm)[i].at[nx - 1]
+        first_stop = jnp.maximum(ix - turn + 1 + place, 0)
+        goal = jnp.minimum(ix + turn - place, sx - 1)
+        leading.append(remote(5 + sy + i, source, through, (first_stop, iy)))
+        follows.append(remote(7 + sy + i, through, plane.at[i], (goal, iy), got=i))
+
+    pl.when(to_x & jnp.logical_not(leads | yields))(plane_w.start)
+
+    @pl.when(leads)
+    def _():
+        for copy in leading:
+            copy.start()
+
     for load in loads[4:]:
         load.start()
 
@@ -357,10 +371,11 @@
 
     pl.when(to_x)(x3.start)
     pl.when(to_xy)(corner.start)
-    pl.when(to_y)(row.start)
-
-    pl.when(to_x & jnp.logical_not(leads))(plane_a.start)
+    pl.when(to_y & jnp.logical_not(leads))(row.start)
+
+    pl.when(to_x & jnp.logical_not(leads | yields))(plane_a.start)
     pl.when(to_x)(x2.start)
+    pl.when(to_y & leads)(row.start)
 
     loads[4].wait()
     loads[5].wait()
@@ -380,42 +395,15 @@
 
     lax.fori_loop(0, 6, own_level_one, 0)
 
+    @pl.when(yields)
+    def _():
+        plane_w.start()
+        plane_a.start()
+
     pl.when(from_y)(row.wait_recv)
-    pl.when(from_xy)(corner.wait_recv)
-    pl.when(from_x)(x3.wait_recv)
-    for part in range(2):
-        k3[part, 0:16] = x3_got[part * 16 : part * 16 + 16]
-        k3[part, 16:20] = row_got[96 + part * 4 : 96 + part * 4 + 4]
-        k3[part, 20:24] = corner_got[24 + part * 4 : 24 + part * 4 + 4]
-        k3[part, 24:32] = jnp.zeros((8, 128), F32)
-        high, low = split(k3[part])
-        grid = later_z_ref[1, nz : nz + 16, 0:128]
-        if part == 1:
-            grid = jnp.zeros_like(grid)
-        rest = jnp.concatenate([high, low, grid, jnp.zeros((48, 128), BF16)], axis=0)
-        own = t3[part] + dot(later_ref[192:224, cells:], rest)
-        blocks[iy, part * 24 : part * 24 + 24] = own[0:24]
-    for copy in gathers:
-        copy.start()
-
-    for part in range(2):
-        k2[part, 0:32] = jnp.zeros((32, nz // 2), F32)
-        for e in range(2):
-            lanes = slice(e * 128, e * 128 + 128)
-            k2[part, 32:40, lanes] = row_got[64 + e * 16 + part * 8 : 64 + e * 16 + part * 8 + 8]
-            k2[part, 40:44, lanes] = corner_got[8 + e * 8 + part * 4 : 8 + e * 8 + part * 4 + 4]
-        k2[part, 44:48] = jnp.zeros((4, nz // 2), F32)
-        high, low = split(k2[part])
-        grid = later_z_ref[0, nz : nz + 16]
-        if part == 1:
-            grid = jnp.zeros_like(grid)
-        rest = jnp.concatenate([high, low, grid, jnp.zeros((16, nz // 2), BF16)], axis=0)
-        t2_ref[part] = t2[part] + dot(later_ref[0:144, cells:], rest)
-
     for part in range(2):
         rows = jnp.concatenate([row_got[part * 32 + c * 8 : part * 32 + c * 8 + 8] for c in range(nz // 128)], axis=1)
-        last = jnp.concatenate([corner_got[part * 4 + c : part * 4 + c + 1] for c in range(nz // 128)], axis=1)
-        edge[part] = jnp.concatenate([rows, last, jnp.zeros((7, nz), F32)], axis=0)
+        edge[part] = jnp.concatenate([rows, jnp.zeros((8, nz), F32)], axis=0)
     high, low = split(edge[...].reshape(32, nz))
     both = jnp.concatenate([high, low], axis=0)
     gap = jnp.zeros((32, nz // 2), BF16)
@@ -432,10 +420,46 @@
             add = dot(table[0:2, 0:2, 1:].reshape(-1, 128), rest).reshape(2, 2, nx // 2 - 1, ny // 2, nz // 2)
             one_ref[part, 0:2, 0:2, a, 1:, 0:8] += add[:, :, :, 0:8]
 
-    @pl.when(helps)
-    def _():
-        lead.wait_recv()
-        follow.start()
+    pl.when(from_xy)(corner.wait_recv)
+    pl.when(from_x)(x3.wait_recv)
+    for part in range(2):
+        k3[part, 0:16] = x3_got[part * 16 : part * 16 + 16]
+        k3[part, 16:20] = row_got[96 + part * 4 : 96 + part * 4 + 4]
+        k3[part, 20:24] = corner_got[24 + part * 4 : 24 + part * 4 + 4]
+        k3[part, 24:32] = jnp.zeros((8, 128), F32)
+        high, low = split(k3[part])
+        grid = later_z_ref[1, nz : nz + 16, 0:128]
+        if part == 1:
+            grid = jnp.zeros_like(grid)
+        rest = jnp.concatenate([high, low, grid, jnp.zeros((48, 128), BF16)], axis=0)
+        own = t3[part] + dot(later_ref[192:224, cells:], rest)
+        blocks[iy, part * 24 : part * 24 + 24] = own[0:24]
+    for copy in gathers:
+        copy.start()
+
+    for part in range(2):
+        edge[part, 8:9] = jnp.concatenate([corner_got[part * 4 + c : part * 4 + c + 1] for c in range(nz // 128)], axis=1)
+
+    for part in range(2):
+        k2[part, 0:32] = jnp.zeros((32, nz // 2), F32)
+        for e in range(2):
+            lanes = slice(e * 128, e * 128 + 128)
+            k2[part, 32:40, lanes] = row_got[64 + e * 16 + part * 8 : 64 + e * 16 + part * 8 + 8]
+            k2[part, 40:44, lanes] = corner_got[8 + e * 8 + part * 4 : 8 + e * 8 + part * 4 + 4]
+        k2[part, 44:48] = jnp.zeros((4, nz // 2), F32)
+        high, low = split(k2[part])
+        grid = later_z_ref[0, nz : nz + 16]
+        if part == 1:
+            grid = jnp.zeros_like(grid)
+        rest = jnp.concatenate([high, low, grid, jnp.zeros((16, nz // 2), BF16)], axis=0)
+        t2_ref[part] = t2[part] + dot(later_ref[0:144, cells:], rest)
+
+    for i in range(2):
+
+        @pl.when(helps[i])
+        def _(i=i):
+            leading[i].wait_recv()
+            follows[i].start()
 
     @pl.when(from_x)
     def _():
@@ -451,14 +475,24 @@
     pl.when(to_y)(row.wait_send)
     pl.when(to_xy)(corner.wait_send)
 
-    pl.when(to_x & jnp.logical_not(leads))(plane_a.wait_send)
-    pl.when(leads)(lead.wait_send)
-    pl.when(helps)(follow.wait_send)
+
+    @pl.when(to_x & jnp.logical_not(leads))
+    def _():
+        plane_w.wait_send()
+        plane_a.wait_send()
+
+    @pl.when(leads)
+    def _():
+        for copy in leading:
+            copy.wait_send()
+
+    for i in range(2):
+        pl.when(helps[i])(follows[i].wait_send)
 
     @pl.when(to_x)
     def _():
-        for copy in (plane_w, x3, x2):
-            copy.wait_send()
+        x3.wait_send()
+        x2.wait_send()
 
 
 def result_kernel(
@@ -586,8 +620,8 @@
                 pltpu.VMEM((2, nz // 128, nx, 128), F32),
                 pltpu.VMEM((ny, nz), F32),
                 pltpu.SemaphoreType.DMA((7,)),
-                pltpu.SemaphoreType.DMA((7 + sy,)),
-                pltpu.SemaphoreType.DMA((7 + sy,)),
+                pltpu.SemaphoreType.DMA((9 + sy,)),
+                pltpu.SemaphoreType.DMA((9 + sy,)),
             ],
             compiler_params=pltpu.CompilerParams(
                 collective_id=0, has_side_effects=True, vmem_limit_bytes=32 * 1024 * 1024

time: 28.3 us -> 27.2 us (0.961); the launches traced: 28.2 us -> 26.8 us
  Pallas kernels: 27.6 us -> 26.2 us
    pallas_call x1, Pallas kernels: 25.1 us -> 23.7 us  [local(): pl.pallas_call(functools.partial(halo_kernel, sx, sy), out_shape=(level_o...]
where the time goes in v4:
time: 27.2 us; the launch traced here: 26.8 us
  Pallas kernels  26.2 us (96%)
  between operations  0.64 us (2%)
    pallas_call x1, Pallas kernels, local(): pl.pallas_call(functools.partial(halo_kernel, sx, sy), out_shape=(level_o...  23.7 us
    pallas_call x1, Pallas kernels, local(): pl.pallas_call(result_kernel, out_shape=(level_one, level_two, level_thre...  2.49 us

profile of v4, /device:TPU:7, one launch (start us, length us, event | category | flops | bytes accessed | tf_op | source)
XLA Modules:
  0.0 26.8 jit_solution(15292176165482196421)
XLA Ops:
  0.6 23.7 %shard_map.85 = (f32[2,3,3,3,4,16,256]{6,5,4,3,2,1,0:T(8,128)S(1)}, f32[2,144,256]{2,1,0:T(8,128)S(1)}, f32[64,256]{1,0:T(8,128)S(1)}, f32[4,48,128]{2,1,0:T(8,1...) custom-call(f32[8,32,512]{2,1,0:T(8,128)} %w_hbm.1, ...), custom_call_target="tpu_custom_call" | custom-call | tf_op jit(solution)/shard_map/pallas_call | solution.py:587
  24.3 2.5 %shard_map.86 = (f32[2,3,3,3,4,16,256]{6,5,4,3,2,1,0:T(8,128)}, f32[2,3,3,3,2,8,128]{6,5,4,3,2,1,0:T(8,128)}, f32[2,3,3,3,1,16,64]{6,5,4,3,2,1,0:T(8,128)}) custom-call(f32[2,3,3,3,4,16,256]{6,5,4,3,2,1,0:T(8,128)S(1)} %get-tuple-element.12.one_ref, f32[2,144,256]{2,1,0:T(8,128)S(1)} %get-tuple-element.13.t2_ref, f32[64,256]{1,0:T(8,128)S(1)} %get-tuple-element.14.x2_ref, ...), custom_call_target="tpu_custom_call" | custom-call | tf_op jit(solution)/shard_map/pallas_call | solution.py:630

commit v5 on v4

--- a/solution.py
+++ b/solution.py
@@ -333,8 +333,6 @@
         for copy in leading:
             copy.start()
 
-    for load in loads[4:]:
-        load.start()
 
     loads[0].wait()
     loads[1].wait()
@@ -348,21 +346,24 @@
                 raw[part, c, x : x + 1] = value[ny - 1 : ny, c * 128 : (c + 1) * 128]
     loads[2].wait()
     loads[3].wait()
-
-    for part in range(2):
-        table = later_ref[:, 0:cells]
+    for load in loads[4:]:
+        load.start()
+
+    def halves(left, right):
+        both = dot(jnp.concatenate(split(left), axis=0), right)
+        return both[: left.shape[0]] + both[left.shape[0] :]
+
+    for part in range(2):
+        table = later_ref[144:320, 0:cells]
         rows = dot(table, mass[part, 0]) + dot(table, mass[part, 1])
-        high, low = split(rows[0:192])
-        two = dot(high, later_z_ref[0, 0:nz]) + dot(low, later_z_ref[0, 0:nz])
-        high, low = split(rows[192:256] + rows[256:320])
-        three = dot(high, later_z_ref[1, 0:nz, 0:128]) + dot(low, later_z_ref[1, 0:nz, 0:128])
-        t2[part] = two[0:144]
+        three = halves(rows[48:112] + rows[112:176], later_z_ref[1, 0:nz, 0:128])
+        two = halves(rows[0:48], later_z_ref[0, 0:nz])
         t3[part] = three[0:32]
         x3_send[part * 16 : part * 16 + 16] = three[32:48]
-        x2_send[part * 32 : part * 32 + 32] = two[144:176]
+        x2_send[part * 32 : part * 32 + 32] = two[0:32]
         for e in range(2):
-            row_send[64 + e * 16 + part * 8 : 64 + e * 16 + part * 8 + 8] = two[176:184, e * 128 : e * 128 + 128]
-            corner_send[8 + e * 8 + part * 4 : 8 + e * 8 + part * 4 + 4] = two[184:188, e * 128 : e * 128 + 128]
+            row_send[64 + e * 16 + part * 8 : 64 + e * 16 + part * 8 + 8] = two[32:40, e * 128 : e * 128 + 128]
+            corner_send[8 + e * 8 + part * 4 : 8 + e * 8 + part * 4 + 4] = two[40:44, e * 128 : e * 128 + 128]
         row_send[96 + part * 4 : 96 + part * 4 + 4] = three[48:52]
         corner_send[24 + part * 4 : 24 + part * 4 + 4] = three[52:56]
         for c in range(nz // 128):
@@ -377,14 +378,19 @@
     pl.when(to_x)(x2.start)
     pl.when(to_y & leads)(row.start)
 
+    for part in range(2):
+        table = later_ref[0:144, 0:cells]
+        rows = dot(table, mass[part, 0]) + dot(table, mass[part, 1])
+        t2[part] = halves(rows, later_z_ref[0, 0:nz])
+
     loads[4].wait()
     loads[5].wait()
 
     def own_level_one(i, carry):
         part, a = i // 3, lax.rem(i, 3)
         table = z_ref[a]
-        z = dot(mass[part, 0], table[0:nz]) + dot(mass[part, 1], table[0:nz])
-        high, low = split(z)
+        both = dot(mass[part].reshape(2 * cells, nz), table[0:nz])
+        high, low = split(both[0:cells] + both[cells:])
         grid = jnp.where(part == 0, table[nz : nz + 16], jnp.zeros((16, nz // 2), BF16))
         rest = jnp.concatenate([jnp.zeros((2 * HALO, nz // 2), BF16), grid, jnp.zeros((16, nz // 2), BF16)], axis=0)
         for ax in range(3):
@@ -511,26 +517,6 @@
             )
     for copy in copies:
         copy.start()
-
-    w, a = plane[0], plane[1]
-    value = jnp.concatenate([-(w + 0.5 * a), edge[0], 0.5 * w - a, edge[1]], axis=0)
-    high, low = split(value)
-    both = jnp.concatenate([high, low], axis=0)
-    half = 2 * HALO
-    for a in range(3):
-        z = dot(both, z_ref[a, 0:nz])
-        zh, zl = split(z[0:half] + z[half:])
-        for part in range(2):
-            own = slice(part * HALO, part * HALO + HALO)
-            rest = jnp.concatenate([zh[own], zl[own], jnp.zeros((32, nz // 2), BF16)], axis=0)
-            add = dot(head_ref[...], rest)
-            first[part, :, :, a] = one_ref[part, 0:2, :, a, 0] + add.reshape(2, 3, -1, nz // 2)
-    for part in range(2):
-        for a in range(2):
-            slot = sem.at[6 + 2 * part + a]
-            copy = pltpu.make_async_copy(first.at[part, a], one_hbm.at[part, a, :, :, 0], slot)
-            copy.start()
-            copies.append(copy)
 
     _, _, _, _, m, n, depth = two.shape
     for part in range(2):
@@ -566,6 +552,26 @@
         three[part, :, :, 0] = lower[:, 0:64].reshape(shape)
     copies.append(pltpu.make_async_copy(three, three_hbm, sem.at[11]))
     copies[-1].start()
+    w, a = plane[0], plane[1]
+    value = jnp.concatenate([-(w + 0.5 * a), edge[0], 0.5 * w - a, edge[1]], axis=0)
+    high, low = split(value)
+    both = jnp.concatenate([high, low], axis=0)
+    half = 2 * HALO
+    for a in range(3):
+        z = dot(both, z_ref[a, 0:nz])
+        zh, zl = split(z[0:half] + z[half:])
+        for part in range(2):
+            own = slice(part * HALO, part * HALO + HALO)
+            rest = jnp.concatenate([zh[own], zl[own], jnp.zeros((32, nz // 2), BF16)], axis=0)
+            add = dot(head_ref[...], rest)
+            first[part, :, :, a] = one_ref[part, 0:2, :, a, 0] + add.reshape(2, 3, -1, nz // 2)
+    for part in range(2):
+        for a in range(2):
+            slot = sem.at[6 + 2 * part + a]
+            copy = pltpu.make_async_copy(first.at[part, a], one_hbm.at[part, a, :, :, 0], slot)
+            copy.start()
+            copies.append(copy)
+
     for copy in copies:
         copy.wait()
 

time: 27.2 us -> 27.2 us (level)
  no operation moved by 1% of the time
where the time goes in v5:
time: 27.2 us; the launch traced here: 26.7 us
  Pallas kernels  26.1 us (96%)
  between operations  0.64 us (2%)
    pallas_call x1, Pallas kernels, local(): pl.pallas_call(functools.partial(halo_kernel, sx, sy), out_shape=(level_o...  23.6 us
    pallas_call x1, Pallas kernels, local(): pl.pallas_call(result_kernel, out_shape=(level_one, level_two, level_thre...  2.42 us

profile of v5, /device:TPU:7, one launch (start us, length us, event | category | flops | bytes accessed | tf_op | source)
XLA Modules:
  0.0 26.7 jit_solution(11825973661184952705)
XLA Ops:
  0.6 23.6 %shard_map.85 = (f32[2,3,3,3,4,16,256]{6,5,4,3,2,1,0:T(8,128)S(1)}, f32[2,144,256]{2,1,0:T(8,128)S(1)}, f32[64,256]{1,0:T(8,128)S(1)}, f32[4,48,128]{2,1,0:T(8,1...) custom-call(f32[8,32,512]{2,1,0:T(8,128)} %w_hbm.1, ...), custom_call_target="tpu_custom_call" | custom-call | tf_op jit(solution)/shard_map/pallas_call | solution.py:593
  24.3 2.4 %shard_map.86 = (f32[2,3,3,3,4,16,256]{6,5,4,3,2,1,0:T(8,128)}, f32[2,3,3,3,2,8,128]{6,5,4,3,2,1,0:T(8,128)}, f32[2,3,3,3,1,16,64]{6,5,4,3,2,1,0:T(8,128)}) custom-call(f32[2,3,3,3,4,16,256]{6,5,4,3,2,1,0:T(8,128)S(1)} %get-tuple-element.12.one_ref, f32[2,144,256]{2,1,0:T(8,128)S(1)} %get-tuple-element.13.t2_ref, f32[64,256]{1,0:T(8,128)S(1)} %get-tuple-element.14.x2_ref, ...), custom_call_target="tpu_custom_call" | custom-call | tf_op jit(solution)/shard_map/pallas_call | solution.py:636

commit v6 on v5

--- a/solution.py
+++ b/solution.py
@@ -375,7 +375,7 @@
     pl.when(to_y & jnp.logical_not(leads))(row.start)
 
     pl.when(to_x & jnp.logical_not(leads | yields))(plane_a.start)
-    pl.when(to_x)(x2.start)
+    pl.when(to_x & jnp.logical_not(yields))(x2.start)
     pl.when(to_y & leads)(row.start)
 
     for part in range(2):
@@ -403,6 +403,7 @@
 
     @pl.when(yields)
     def _():
+        x2.start()
         plane_w.start()
         plane_a.start()
 

time: 27.2 us -> 27.2 us (level)
  no operation moved by 1% of the time
where the time goes in v6:
time: 27.2 us; the launch traced here: 26.7 us
  Pallas kernels  26.1 us (96%)
  between operations  0.64 us (2%)
    pallas_call x1, Pallas kernels, local(): pl.pallas_call(functools.partial(halo_kernel, sx, sy), out_shape=(level_o...  23.6 us
    pallas_call x1, Pallas kernels, local(): pl.pallas_call(result_kernel, out_shape=(level_one, level_two, level_thre...  2.42 us

profile of v6, /device:TPU:7, one launch (start us, length us, event | category | flops | bytes accessed | tf_op | source)
XLA Modules:
  0.0 26.7 jit_solution(7444868186083203661)
XLA Ops:
  0.6 23.6 %shard_map.85 = (f32[2,3,3,3,4,16,256]{6,5,4,3,2,1,0:T(8,128)S(1)}, f32[2,144,256]{2,1,0:T(8,128)S(1)}, f32[64,256]{1,0:T(8,128)S(1)}, f32[4,48,128]{2,1,0:T(8,1...) custom-call(f32[8,32,512]{2,1,0:T(8,128)} %w_hbm.1, ...), custom_call_target="tpu_custom_call" | custom-call | tf_op jit(solution)/shard_map/pallas_call | solution.py:594
  24.3 2.4 %shard_map.86 = (f32[2,3,3,3,4,16,256]{6,5,4,3,2,1,0:T(8,128)}, f32[2,3,3,3,2,8,128]{6,5,4,3,2,1,0:T(8,128)}, f32[2,3,3,3,1,16,64]{6,5,4,3,2,1,0:T(8,128)}) custom-call(f32[2,3,3,3,4,16,256]{6,5,4,3,2,1,0:T(8,128)S(1)} %get-tuple-element.12.one_ref, f32[2,144,256]{2,1,0:T(8,128)S(1)} %get-tuple-element.13.t2_ref, f32[64,256]{1,0:T(8,128)S(1)} %get-tuple-element.14.x2_ref, ...), custom_call_target="tpu_custom_call" | custom-call | tf_op jit(solution)/shard_map/pallas_call | solution.py:637
